TPU v7x, 128 devices: a whole 4x4x4 slice. The times are simulated.
128 devices in a mesh: box: 16 (over y, x_hi, core), blk: 8 (over x_lo, z).
Axes of the slice: x: 4 (x_hi: 2, x_lo: 2; x = x_hi * 2 + x_lo), y: 4, z: 4, core: 2. Of those that a mesh axis runs over, the one named last changes fastest.
Arguments:
- interface_rows: float32 [2, 16, 256, 1024], P(None, 'box', 'blk'), as said below
- exterior_rows: float32 [2, 16, 768, 1024], P(None, 'box', 'blk'), as said below
- pml_mask: int32 [2, 16, 1024], P(None, 'box'), may hold values 0 or 1
Outputs:
- level_one: float32 [2, 16, 768, 1536], P(None, 'box', 'blk')
- level_two: float32 [2, 16, 384, 1536], P(None, 'box', 'blk')
Inputs may be any that keep to these rules, and one draw needn't show every extreme that they name: `interface_rows`: for every slot and leaf, the matrix formed by its interface rows above its exterior rows is symmetric and positive definite. `exterior_rows`: for every slot and leaf, the matrix formed by its interface rows above its exterior rows is symmetric and positive definite.
All inputs are finite; a program needn't handle non-finite values. No bound on the sum of `pml_mask` on one device may be relied on, other than what follows from the above.
Results may differ from a plain program's by a relative error of at most 0.00005.
Values sent between devices are 32-bit elements; how exact they have to be, the bound alone decides.
No kernel may reach another device: no remote copies, remote signals or barrier semaphores. Data moves between devices by JAX's collectives and lax.ppermute only.
A program may use at most 128 MiB of HBM per device.

v0:
```python
import jax
import jax.numpy as jnp
from jax import lax
from jax.sharding import PartitionSpec as P

SEGMENT = 16


pml_damping = 2.0


def partner(block, axis, distance):
    count = lax.axis_size(axis)
    route = []
    for low in range(count):
        high = low | 1 << distance
        if high != low and high < count:
            route += [(low, high), (high, low)]
    return lax.ppermute(block, axis, route)


def damped(rows, offset, mask_row):
    count = rows.shape[-2]
    width = rows.shape[-1]
    match_table = (jnp.arange(count)[:, None] + offset == jnp.arange(width)[None, :]).astype(
        jnp.float32
    )
    return rows + match_table * (pml_damping * mask_row.astype(jnp.float32))[..., None, :]


def cholesky_solve(factor, right):
    forward = lax.linalg.triangular_solve(
        factor, right, left_side=True, lower=True, transpose_a=False
    )
    return lax.linalg.triangular_solve(
        factor, forward, left_side=True, lower=True, transpose_a=True
    )


def schur_terms(upper_first, upper_second, inner):
    schur = upper_first[..., :inner] + upper_second[..., :inner]
    coupled = jnp.concatenate([upper_first[..., inner:], upper_second[..., inner:]], axis=-1)
    return (jnp.linalg.cholesky(schur), coupled)


def own_correction(factor, lower_rows, coupled, inner):
    right = jnp.swapaxes(lower_rows[..., :inner], 1, 2)
    weights = cholesky_solve(factor, right)
    return jnp.einsum("skr,skc->src", weights, coupled, precision=lax.Precision.HIGHEST)


def place_rows(lower_rows, correction, place_first, inner):
    outer = lower_rows[..., inner:]
    blank = jnp.zeros_like(outer)
    placed = jnp.where(
        place_first,
        jnp.concatenate([outer, blank], axis=-1),
        jnp.concatenate([blank, outer], axis=-1),
    )
    return placed - correction


def reorder(rows, segment):
    width = rows.shape[-1]
    lead = rows.shape[:-1]
    grouped = rows.reshape(lead + (width // (2 * segment), 2, segment))
    shared = grouped[..., 0, :].reshape(lead + (width // 2,))
    others = grouped[..., 1, :].reshape(lead + (width // 2,))
    return jnp.concatenate([shared, others], axis=-1)


def local(interface_rows, exterior_rows, pml_mask):
    blocks = lax.axis_size("blk")
    block_index = lax.axis_index("blk")
    box_index = lax.axis_index("box")
    slot_count = interface_rows.shape[0]
    local_inner = interface_rows.shape[2]
    local_outer = exterior_rows.shape[2]
    inner_count = local_inner * blocks
    mask_row = pml_mask[:, 0]
    inner_rows = damped(interface_rows[:, 0], block_index * local_inner, mask_row)
    outer_rows = damped(exterior_rows[:, 0], inner_count + block_index * local_outer, mask_row)
    first_one = box_index % 2 == 0
    mine_full = lax.all_gather(inner_rows, "blk", axis=1, tiled=True)
    other_full = partner(mine_full, "box", 0)
    upper_first = jnp.where(first_one, mine_full, other_full)
    upper_second = jnp.where(first_one, other_full, mine_full)
    factor, coupled = schur_terms(upper_first, upper_second, inner_count)
    correction = own_correction(factor, outer_rows, coupled, inner_count)
    level_one = place_rows(outer_rows, correction, first_one, inner_count)
    total = level_one.shape[2]
    half_width = total // 2
    grouped = level_one.reshape(slot_count, local_outer // (2 * SEGMENT), 2, SEGMENT, total)
    shared_local = reorder(grouped[:, :, 0].reshape(slot_count, local_outer // 2, total), SEGMENT)
    other_local = reorder(grouped[:, :, 1].reshape(slot_count, local_outer // 2, total), SEGMENT)
    gathered = lax.all_gather(shared_local, "blk", axis=1, tiled=True)
    partner_half = partner(gathered, "box", 0)
    mine_box = jnp.where(
        first_one,
        jnp.concatenate([gathered, partner_half], axis=1),
        jnp.concatenate([partner_half, gathered], axis=1),
    )
    other_box = partner(mine_box, "box", 1)
    first_two = box_index // 2 % 2 == 0
    upper_first_two = jnp.where(first_two, mine_box, other_box)
    upper_second_two = jnp.where(first_two, other_box, mine_box)
    factor_two, coupled_two = schur_terms(upper_first_two, upper_second_two, half_width)
    correction_two = own_correction(factor_two, other_local, coupled_two, half_width)
    level_two = place_rows(other_local, correction_two, first_two, half_width)
    return (level_one[:, None], level_two[:, None])


def solution(mesh):
    in_specs = (P(None, "box", "blk", None), P(None, "box", "blk", None), P(None, "box", None))
    out_specs = (P(None, "box", "blk", None), P(None, "box", "blk", None))
    return jax.shard_map(local, mesh=mesh, in_specs=in_specs, out_specs=out_specs, check_vma=False)
```

profile of v0, /device:TPU:1, one launch (start us, length us, event | category | flops | bytes accessed | tf_op | source)
XLA Modules:
  0.0 1000.5 jit_solution(13607873520543579445)
XLA Ops:
  8.1 1.9 bitcast_add_fusion.3
  10.1 39.8 %all-gather.3.cloned.1.call-done = f32[2,256,1024]{2,0,1:T(2,128)} async-done(((f32[2,32,1024]{2,0,1:T(2,128)}), f32[2,256,1024]{2,0,1:T(2,128)}) %all-gather.3.cloned.1.call-update) | async-done | bytes 2097168 | tf_op jit(solution)/shard_map/all_gather | solution.py:84
  49.9 2.7 copy.190
  52.6 6.2 collective-permute-start
  60.7 2.1 collective-permute-done
  62.8 2.0 broadcast_select_fusion.3
  65.8 2.0 copy.192
  70.6 24.3 %custom-call.65 = f32[2,128,128]{2,1,0:T(8,128)S(1)} custom-call(f32[2,128,128]{2,1,0:T(8,128)} %cholesky.497), custom_call_target="Cholesky" | custom-call | tf_op jit(solution)/shard_map/jit(cholesky)/cholesky | solution.py:43
  96.4 21.1 %custom-call.80 = f32[2,1,128,128]{2,3,1,0:T(8,128)} custom-call(f32[2,1,128,128]{3,2,1,0:T(8,128)} %select_bitcast_fusion.1), custom_call_target="InvertDiagBlocksLowerTriangular" | custom-call | tf_op jit(solution)/shard_map/jit(cholesky)/cholesky/custom-call.1 | solution.py:43
  117.5 1.9 constant_dynamic-update-slice_fusion.22
  119.4 1.9 convolution_subtract_fusion
  121.3 24.9 %custom-call.66 = f32[2,128,128]{2,1,0:T(8,128)} custom-call(f32[2,128,128]{2,1,0:T(8,128)} %convolution_subtract_fusion), custom_call_target="Cholesky" | custom-call | tf_op jit(solution)/shard_map/jit(cholesky)/cholesky | solution.py:43
  147.9 2.0 select_select_fusion.1
  150.0 7.2 while.2
  150.7 3.0 bitcast_dynamic-update-slice_fusion.4
  154.3 2.9 bitcast_dynamic-update-slice_fusion.4
  157.2 40.3 %custom-call.67 = f32[2,2,128,128]{2,3,1,0:T(8,128)S(1)} custom-call(f32[2,2,128,128]{3,2,1,0:T(8,128)} %bitcast.199), custom_call_target="InvertDiagBlocksLowerTriangular" | custom-call | tf_op jit(solution)/shard_map/triangular_solve | solution.py:35
  202.3 4.5 fusion.9
  208.8 8.0 reshape_reshape_squeeze.7
  216.8 10.0 %fusion.128 = (f32[2,48,48,1,16]{4,3,2,1,0:T(1,128)}, f32[2,48,48,1,16]{4,3,2,1,0:T(1,128)S(1)}) fusion(f32[2,48,48,2,16]{4,3,2,1,0:T(2,128)} %reshape_reshape_squeeze.7), kind=kLoop, calls=%fused_computation.227 | loop fusion | bytes 1179648 | tf_op jit(solution)/shard_map/slice | solution.py:67
  226.8 4.7 copy.206
  231.5 3.5 copy.207
  237.6 56.5 %all-gather.5.cloned.1.call-done = f32[2,384,1536]{2,0,1:T(2,128)} async-done(((f32[2,48,1536]{2,0,1:T(2,128)}), f32[2,384,1536]{2,0,1:T(2,128)}) %all-gather.5.cloned.1.call-update) | async-done | bytes 4718608 | tf_op jit(solution)/shard_map/all_gather | solution.py:96
  294.2 8.2 copy.210
  303.0 7.7 collective-permute-done.1
  310.8 8.7 maximum_select_fusion
  319.5 2.4 collective-permute-start.2
  322.9 7.9 reshape_reshape_squeeze.6
  330.8 10.1 %fusion.127 = (f32[2,48,48,1,16]{4,3,2,1,0:T(1,128)S(1)}, f32[2,48,48,1,16]{4,3,2,1,0:T(1,128)}) fusion(f32[2,48,48,2,16]{4,3,2,1,0:T(2,128)} %reshape_reshape_squeeze.6), kind=kLoop, calls=%fused_computation.226 | loop fusion | bytes 1179648 | tf_op jit(solution)/shard_map/slice | solution.py:68
  340.8 4.7 copy.224
  348.4 177.1 %collective-permute-done.2 = f32[2,768,1536]{1,2,0:T(8,128)} collective-permute-done((f32[2,768,1536]{1,2,0:T(8,128)}, f32[2,768,1536]{1,2,0:T(8,128)}, u32[]{:S(2)}, u32[]{:S(2)}) %collective-permute-start.2) | collective-permute-done | bytes 9437216 | tf_op jit(solution)/shard_map/ppermute | solution.py:19
  525.5 7.1 broadcast_select_fusion.1
  532.6 5.3 fusion.126
  537.9 6.1 copy.212
  543.9 4.4 fusion.4
  548.3 2.2 copy-done
  550.6 23.7 %custom-call.68 = f32[2,128,128]{2,1,0:T(8,128)S(1)} custom-call(f32[2,128,128]{2,1,0:T(8,128)S(1)} %cholesky.500), custom_call_target="Cholesky" | custom-call | tf_op jit(solution)/shard_map/jit(cholesky)/cholesky | solution.py:43
  574.2 2.4 cholesky.425
  576.7 19.7 %custom-call.69 = f32[2,1,128,128]{2,3,1,0:T(8,128)S(1)} custom-call(f32[2,1,128,128]{3,2,1,0:T(8,128)S(1)} %select_bitcast_fusion.5), custom_call_target="InvertDiagBlocksLowerTriangular" | custom-call | tf_op jit(solution)/shard_map/jit(cholesky)/cholesky | solution.py:43
  596.4 2.7 constant_dynamic-update-slice_fusion.20
  600.9 23.5 %custom-call.70 = f32[2,128,128]{2,1,0:T(8,128)S(1)} custom-call(f32[2,128,128]{2,1,0:T(8,128)S(1)} %cholesky.504), custom_call_target="Cholesky" | custom-call | tf_op jit(solution)/shard_map/jit(cholesky)/cholesky | solution.py:43
  625.1 20.1 %custom-call.71 = f32[2,1,128,128]{2,3,1,0:T(8,128)S(1)} custom-call(f32[2,1,128,128]{3,2,1,0:T(8,128)S(1)} %get-tuple-element.77), custom_call_target="InvertDiagBlocksLowerTriangular" | custom-call | tf_op jit(solution)/shard_map/jit(cholesky)/cholesky | solution.py:43
  646.6 2.5 slice_subtract_fusion.1
  649.1 23.5 %custom-call.72 = f32[2,128,128]{2,1,0:T(8,128)S(1)} custom-call(f32[2,128,128]{2,1,0:T(8,128)S(1)} %cholesky.509), custom_call_target="Cholesky" | custom-call | tf_op jit(solution)/shard_map/jit(cholesky)/cholesky | solution.py:43
  673.2 19.7 %custom-call.73 = f32[2,1,128,128]{2,3,1,0:T(8,128)S(1)} custom-call(f32[2,1,128,128]{3,2,1,0:T(8,128)S(1)} %get-tuple-element.75), custom_call_target="InvertDiagBlocksLowerTriangular" | custom-call | tf_op jit(solution)/shard_map/jit(cholesky)/cholesky | solution.py:43
  694.2 2.7 slice_subtract_fusion.2
  696.9 23.6 %custom-call.74 = f32[2,128,128]{2,1,0:T(8,128)S(1)} custom-call(f32[2,128,128]{2,1,0:T(8,128)S(1)} %cholesky.514), custom_call_target="Cholesky" | custom-call | tf_op jit(solution)/shard_map/jit(cholesky)/cholesky | solution.py:43
  721.3 19.7 %custom-call.75 = f32[2,1,128,128]{2,3,1,0:T(8,128)S(1)} custom-call(f32[2,1,128,128]{3,2,1,0:T(8,128)S(1)} %get-tuple-element.73), custom_call_target="InvertDiagBlocksLowerTriangular" | custom-call | tf_op jit(solution)/shard_map/jit(cholesky)/cholesky | solution.py:43
  742.0 2.5 slice_subtract_fusion.3
  744.6 23.5 %custom-call.76 = f32[2,128,128]{2,1,0:T(8,128)S(1)} custom-call(f32[2,128,128]{2,1,0:T(8,128)S(1)} %cholesky.519), custom_call_target="Cholesky" | custom-call | tf_op jit(solution)/shard_map/jit(cholesky)/cholesky | solution.py:43
  768.7 19.9 %custom-call.81 = f32[2,1,128,128]{2,3,1,0:T(8,128)S(1)} custom-call(f32[2,1,128,128]{3,2,1,0:T(8,128)S(1)} %get-tuple-element.71), custom_call_target="InvertDiagBlocksLowerTriangular" | custom-call | tf_op jit(solution)/shard_map/jit(cholesky)/cholesky/custom-call.1 | solution.py:43
  789.5 2.2 slice_subtract_fusion.4
  791.8 23.5 %custom-call.77 = f32[2,128,128]{2,1,0:T(8,128)S(1)} custom-call(f32[2,128,128]{2,1,0:T(8,128)S(1)} %slice_subtract_fusion.4), custom_call_target="Cholesky" | custom-call | tf_op jit(solution)/shard_map/jit(cholesky)/cholesky | solution.py:43
  816.7 5.3 select_select_fusion
  822.0 20.6 %while.3 = (s32[]{:T(128)}, f32[2,768,768]{2,1,0:T(8,128)}, s32[6,2]{0,1:T(2,128)S(1)}, f32[6,2,128,128]{3,2,0,1:T(8,128)}, s32[]{:T(128)}) while((s32[]{:T(128)}, f32[2,768,768]{2,1,0:T(8,128)}, s32[6,2]{0,1:T(2,128)S(1)}, f32[6,2,128,128]{3,2,0,1:T(8,128)}, s32[]{:T(128)}) %tuple.74), condition=%wide.while_cond.1, body=%wide.while_body.1.sunk | while | flops 2 | bytes 263777 | solution.py:35
  822.6 2.8 bitcast_dynamic-update-slice_fusion.5
  826.1 2.9 bitcast_dynamic-update-slice_fusion.5
  829.5 2.9 bitcast_dynamic-update-slice_fusion.5
  833.0 2.8 bitcast_dynamic-update-slice_fusion.5
  836.4 2.8 bitcast_dynamic-update-slice_fusion.5
  839.9 2.8 bitcast_dynamic-update-slice_fusion.5
  842.7 119.0 %custom-call.78 = f32[2,6,128,128]{2,3,1,0:T(8,128)S(1)} custom-call(f32[2,6,128,128]{3,2,1,0:T(8,128)} %bitcast.198), custom_call_target="InvertDiagBlocksLowerTriangular" | custom-call | tf_op jit(solution)/shard_map/triangular_solve | solution.py:35
  968.8 2.0 convolution_subtract_fusion.6
  980.0 13.3 %fusion.15 = f32[2,1,48,1536]{3,2,1,0:T(8,128)} fusion(f32[2,768,48]{1,2,0:T(8,128)S(1)} %constant_dynamic-update-slice_fusion.10, f32[2,768,768]{1,2,0:T(8,128)} %get-tuple-element.61, f32[2,768,768]{1,2,0:T(8,128)} %get-tuple-element.59, f32[2,48,768]{2,1,0:T(8,128)S(1)} %copy.203, pred[]{:T(512)S(6)} %eq.50), kind=kOutput, calls=%fused_computation.21 | convolution fusion | flops 1361608704 | bytes 10616833 | tf_op jit(solution)/shard_map/skr,skc->src/dot_general | solution.py:49
  (128 shorter events, 55.7 us)
Async XLA Ops:
  7.2 51.8 %copy-start.6 = (f32[2,1,96,1024]{3,2,1,0:T(8,128)S(1)}, f32[2,1,96,1024]{3,2,1,0:T(8,128)}, u32[]{:S(2)}) copy-start(f32[2,1,96,1024]{3,2,1,0:T(8,128)} %param.6) | copy-start | bytes 2359300
  7.2 42.7 %all-gather.3.cloned.1.call-start = ((), (), s32[]{:S(2)}) async-start(), calls=%async_computation | async-start | bytes 2359296 | tf_op jit(solution)/shard_map/all_gather | solution.py:84
  10.0 284.1 %all-gather.5.cloned.1.call-start = ((), (), s32[]{:S(2)}) async-start(), calls=%async_computation.1 | async-start | bytes 5308416 | tf_op jit(solution)/shard_map/all_gather | solution.py:96
  52.6 10.2 %collective-permute-start = (f32[2,256,1024]{1,2,0:T(8,128)S(1)}, f32[2,256,1024]{1,2,0:T(8,128)}, u32[]{:S(2)}, u32[]{:S(2)}) collective-permute-start(f32[2,256,1024]{1,2,0:T(8,128)S(1)} %copy.190), channel_id=1, source_target_pairs={{0,8},{8,0},{16,24},{24,16},{32,40},{40,32},{48,56},{56,48},{64,72... | collective-permute-start | bytes 6291464 | tf_op jit(solution)/shard_map/ppermute | solution.py:19
  69.2 0.8 copy-start.4
  206.9 1.0 copy-start.1
  302.3 20.5 %copy-start.3 = (f32[2,3,1,16,1536]{4,3,1,0,2:T(8,128)S(1)}, f32[2,3,1,16,1536]{4,3,1,0,2:T(8,128)}, u32[]{:S(2)}) copy-start(f32[2,3,1,16,1536]{4,3,1,0,2:T(8,128)} %get-tuple-element.68) | copy-start | bytes 1769476
  302.3 8.4 collective-permute-start.1
  319.5 206.0 %collective-permute-start.2 = (f32[2,768,1536]{1,2,0:T(8,128)}, f32[2,768,1536]{1,2,0:T(8,128)}, u32[]{:S(2)}, u32[]{:S(2)}) collective-permute-start(f32[2,768,1536]{1,2,0:T(8,128)} %maximum_select_fusion), channel_id=1, source_target_pairs={{0,16},{16,0},{8,24},{24,8},{32,48},{48,32},{40,56},{56,40},{64,80... | collective-permute-start | bytes 28311560 | tf_op jit(solution)/shard_map/ppermute | solution.py:19
  548.3 2.2 copy-start
  692.9 123.8 %copy-start.2 = (pred[768,768]{1,0:T(8,128)(4,1)S(1)}, pred[768,768]{1,0:T(8,128)(4,1)}, u32[]{:S(2)}) copy-start(pred[768,768]{1,0:T(8,128)(4,1)} %iota_compare_fusion) | copy-start | bytes 1769476
  816.7 144.9 %copy-start.5 = (f32[2,48,768]{2,1,0:T(8,128)S(1)}, f32[2,48,768]{2,1,0:T(8,128)}, u32[]{:S(2)}) copy-start(f32[2,48,768]{2,1,0:T(8,128)} %copy.225) | copy-start | bytes 884740
Sparse Core Ops, SparseCore 0:
  10.2 39.5 all-gather.2
  237.8 56.3 all-gather.4
where the time goes:
time: 1010 us; the launch traced here: 1000 us
  other arithmetic  518 us (51%)
  waiting for transfers between devices  283 us (28%)
  local copies, waits for them, and re-layouts  111 us (11%)
  matrix products  63.7 us (6%)
  between operations  15 us (1%)
    another operation x33, other arithmetic, schur_terms(): return (jnp.linalg.cholesky(schur), coupled)  317 us
    ppermute x3, waiting for transfers between devices, partner(): return lax.ppermute(block, axis, route)  187 us
    another operation x8, other arithmetic, cholesky_solve(): lax.linalg.triangular_solve(factor, forward, left_side=True, lower=True,...  168 us
    all_gather x1, waiting for transfers between devices, local(): gathered = lax.all_gather(shared_local, 'blk', axis=1, tiled=True)  56.5 us
    all_gather x1, waiting for transfers between devices, local(): mine_full = lax.all_gather(inner_rows, 'blk', axis=1, tiled=True)  39.8 us
    another operation x24, local copies, waits for them, and re-layouts  27.9 us
    another operation x12, matrix products, schur_terms(): return (jnp.linalg.cholesky(schur), coupled)  23 us
  transfers between devices with their start and end apart: 5, of which 5 were waited for; matrix products, arithmetic and copies ran while one was open for 3% of the time, Pallas kernels for 0%

commit v1 on v0

v1 whole, which is shorter than its diff:
```python
import functools

import jax
import jax.numpy as jnp
from jax import lax
from jax.experimental import pallas as pl
from jax.experimental.pallas import tpu as pltpu
from jax.sharding import Mesh
from jax.sharding import PartitionSpec as P

HI = lax.Precision.HIGHEST
DAMPING = 2.0
VMEM_LIMIT = 48 * 2**20
PLANE = ("xh", "xl", "z")


def dot(a, b):
    return jnp.dot(a, b, precision=HI, preferred_element_type=jnp.float32)


def dot_nt(a, b):
    return lax.dot_general(
        a, b, (((1,), (1,)), ((), ())), precision=HI, preferred_element_type=jnp.float32
    )


def small_sweep(entries):
    n = len(entries)
    a = [[entries[max(i, j)][min(i, j)] for j in range(n)] for i in range(n)]
    for k in range(n):
        r = 1.0 / a[k][k]
        u = [a[k][j] * r for j in range(n)]
        new = [[None] * n for _ in range(n)]
        for i in range(n):
            for j in range(i + 1):
                if i == k and j == k:
                    v = -r
                elif i == k:
                    v = u[j]
                elif j == k:
                    v = u[i]
                else:
                    v = a[i][j] - a[i][k] * u[j]
                new[i][j] = v
                new[j][i] = v
        a = new
    return a


def tree_sum(t):
    while len(t) > 1:
        t = [t[i] + t[i + 1] for i in range(0, len(t) - 1, 2)] + ([t[-1]] if len(t) % 2 else [])
    return t[0]


def pivot_rows(row, k, lane):
    w = row.shape[1]
    inblk = (lane >= 8 * k) & (lane < 8 * k + 8)
    col = [jnp.broadcast_to(row[:, 8 * k + q : 8 * k + q + 1], (8, w)) for q in range(8)]
    entries = [
        [jnp.broadcast_to(col[j][i : i + 1], (8, w)) if j <= i else None for j in range(8)]
        for i in range(8)
    ]
    m = small_sweep(entries)
    rb = [
        jnp.where(
            inblk,
            jnp.where(lane == 8 * k + j, -1.0, 0.0),
            jnp.broadcast_to(row[j : j + 1], (8, w)),
        )
        for j in range(8)
    ]
    return [tree_sum([m[i][j] * rb[j] for j in range(8)]) for i in range(8)]


def sweep_blocks(mats):
    n = 128
    steps = n // 8
    lane = lax.broadcasted_iota(jnp.int32, (8, n), 1)
    sub = lax.broadcasted_iota(jnp.int32, (8, n), 0)
    full_lane = lax.broadcasted_iota(jnp.int32, (n, n), 1)
    mats = list(mats)
    rows = [a[0:8] for a in mats]
    for k in range(steps):
        inblk = (lane >= 8 * k) & (lane < 8 * k + 8)
        full_in = (full_lane >= 8 * k) & (full_lane < 8 * k + 8)
        next_mats, next_rows = [], []
        for a, row in zip(mats, rows):
            news = pivot_rows(row, k, lane)
            packed = news[7]
            for i in range(7):
                packed = jnp.where(sub == i, news[i], packed)
            if k < steps - 1:
                ahead = a[8 * k + 8 : 8 * k + 16]
                terms = [
                    jnp.broadcast_to(ahead[:, 8 * k + q : 8 * k + q + 1], (8, n)) * news[q]
                    for q in range(8)
                ]
                next_rows.append(jnp.where(inblk, 0.0, ahead) + tree_sum(terms))
            zero = jnp.zeros((8, n), jnp.float32)
            spread = jnp.concatenate([packed if v == k else zero for v in range(steps)], 0)
            full = jnp.where(full_in, 0.0, a) + dot(jnp.where(full_in, a, 0.0), spread)
            parts = ([full[: 8 * k]] if k > 0 else []) + [-packed]
            if k < steps - 1:
                parts.append(next_rows[-1])
                if k < steps - 2:
                    parts.append(full[8 * k + 16 :])
            next_mats.append(jnp.concatenate(parts, 0))
        mats, rows = next_mats, next_rows
    return mats


def sweep_refs(refs, kb):
    at = pl.ds(pl.multiple_of(kb * 128, 128), 128)
    inverses = sweep_blocks([ref[at, at] for ref in refs])
    for ref, x in zip(refs, inverses):
        minus = dot(x, ref[at, :])
        column = ref[:, at]
        side = dot(column, x)
        ref[...] = ref[...] + dot(column, minus)
        ref[at, :] = -minus
        ref[:, at] = -side
        ref[at, at] = x


def lane_index(rows, back):
    lane = lax.broadcasted_iota(jnp.int32, (rows, 128), 1)
    if back:
        seg = lane // 16
        return (seg % 2) * 64 + (seg // 2) * 16 + lane % 16
    half = lane // 64
    return ((lane % 64) // 16) * 32 + half * 16 + lane % 16


def pick(x, index):
    return jnp.take_along_axis(x, index, axis=1)


def split_columns(x):
    rows = x.shape[0]
    index = lane_index(rows, False)
    low = lax.broadcasted_iota(jnp.int32, (rows, 128), 1) < 64
    shared, other = [], []
    for j in range(3):
        a = pick(x[:, 256 * j : 256 * j + 128], index)
        b = pick(x[:, 256 * j + 128 : 256 * j + 256], index)
        shared.append(jnp.where(low, a, pltpu.roll(b, 64, 1)))
        other.append(jnp.where(low, pltpu.roll(a, 64, 1), b))
    return shared + other


def join_columns(panels):
    rows = panels[0].shape[0]
    index = lane_index(rows, True)
    low = lax.broadcasted_iota(jnp.int32, (rows, 128), 1) < 64
    out = []
    for j in range(3):
        s, o = panels[j], panels[3 + j]
        out.append(pick(jnp.where(low, s, pltpu.roll(o, 64, 1)), index))
        out.append(pick(jnp.where(low, pltpu.roll(s, 64, 1), o), index))
    return out


def shared_rows(x):
    return jnp.concatenate([x[0:16], x[32:48], x[64:80]], 0)


def other_rows(x):
    return jnp.concatenate([x[16:32], x[48:64], x[80:96]], 0)


def choose(first, a, b):
    return jnp.where(first, a, b), jnp.where(first, b, a)


def damp_kernel(where_ref, inner_ref, outer_ref, mask_ref, mine_ref, send_ref):
    core, blk = where_ref[0], where_ref[1]
    for out_ref, slot in ((mine_ref, core), (send_ref, 1 - core)):
        gain = DAMPING * mask_ref[slot].astype(jnp.float32)
        for source, start, count, offset in (
            (inner_ref, 0, 32, blk * 32),
            (outer_ref, 32, 96, 256 + blk * 96),
        ):
            row = lax.broadcasted_iota(jnp.int32, (count, 1024), 0) + offset
            lane = lax.broadcasted_iota(jnp.int32, (count, 1024), 1)
            match = jnp.where(row == lane, 1.0, 0.0)
            out_ref[start : start + count, :] = source[slot] + match * gain


def split_kernel(
    where_ref, mine_ref, recv_ref, keep_ref, send_ref, s1_ref, bulk_ref, es_ref, ei_ref, lee_ref
):
    first = where_ref[0] == 0
    upper = where_ref[2] == 0
    boxes = choose(first, mine_ref[...], recv_ref[...])
    total = boxes[0][0:32, 0:256] + boxes[1][0:32, 0:256]
    s1_ref[0] = total[:, 0:128]
    s1_ref[1] = total[:, 128:256]
    kept = []
    for t, box in enumerate(boxes):
        panels = split_columns(box[:, 256:1024])
        for j in range(6):
            bulk_ref[32 * (6 * t + j) : 32 * (6 * t + j) + 32, :] = panels[j][0:32]
        for j in range(3):
            base = 384 + 144 * t + 48 * j
            bulk_ref[base : base + 48, :] = shared_rows(panels[3 + j][32:128])
            es_ref[t, :, 128 * j : 128 * j + 128] = other_rows(panels[j][32:128])
            lee_ref[t, :, 128 * j : 128 * j + 128] = other_rows(panels[3 + j][32:128])
        ei_ref[t] = other_rows(box[32:128, 0:256])
        kept.append([shared_rows(panels[j][32:128]) for j in range(3)])
    for j in range(3):
        keep_ref[j], send_ref[j] = choose(upper, kept[0][j], kept[1][j])


def first_kernel(where_ref, early_ref, d_ref, s_ref, a_ref, b_ref, c_ref):
    pair = where_ref[2]
    row = lax.broadcasted_iota(jnp.int32, (384, 384), 0)
    lane = lax.broadcasted_iota(jnp.int32, (384, 384), 1)
    c_ref[...] = jnp.where(row == lane, 1.0, 0.0)
    for k in range(8):
        for j in range(3):
            at = (slice(48 * k, 48 * k + 48), slice(128 * j, 128 * j + 128))
            a_ref[at] = early_ref[k, 48 * j : 48 * j + 48]
            b_ref[at] = early_ref[8 + k, 48 * j : 48 * j + 48]
        for j in range(2):
            c_ref[32 * k : 32 * k + 32, 128 * j : 128 * j + 128] = early_ref[
                8 * pair + k, 144 + 32 * j : 176 + 32 * j
            ]

    def step(kb, carry):
        sweep_refs([a_ref, b_ref, c_ref], kb)
        return carry

    lax.fori_loop(0, 3, step, 0)
    d_ref[0] = -a_ref[...]
    d_ref[1] = -b_ref[...]
    s_ref[...] = -c_ref[0:256, 0:256]


def one_kernel(where_ref, bulk_ref, s_ref, mine_ref, recv_ref, keep_ref, send_ref, u_ref):
    first = where_ref[0] == 0
    pair = where_ref[2]
    for k in range(8):
        for j in range(12):
            u_ref[32 * k : 32 * k + 32, 128 * j : 128 * j + 128] = bulk_ref[
                8 * pair + k, 32 * j : 32 * j + 32
            ]
    boxes = choose(first, mine_ref[32:128, :], recv_ref[32:128, :])
    left = jnp.concatenate([boxes[0][:, 0:256], boxes[1][:, 0:256]], 0)
    right = dot(dot(left, s_ref[...]), u_ref[...])
    outs = []
    for t in range(2):
        block = right[96 * t : 96 * t + 96]
        panels = []
        for h in range(2):
            part = join_columns(
                [block[:, 768 * h + 128 * j : 768 * h + 128 * j + 128] for j in range(6)]
            )
            for j in range(6):
                if h == t:
                    panels.append(boxes[t][:, 256 + 128 * j : 384 + 128 * j] - part[j])
                else:
                    panels.append(-part[j])
        outs.append(jnp.concatenate(panels, 1))
    keep_ref[...], send_ref[...] = choose(first, outs[0], outs[1])


def two_kernel(
    where_ref,
    bulk_ref,
    early_ref,
    d_ref,
    es_ref,
    ei_ref,
    lee_ref,
    keep_ref,
    send_ref,
    u_ref,
    v_ref,
    c_ref,
    l_ref,
):
    first = where_ref[0] == 0
    upper = where_ref[2] == 0
    for p in range(2):
        for k in range(8):
            at = slice(256 * p + 32 * k, 256 * p + 32 * k + 32)
            for t in range(2):
                for j in range(3):
                    base = 32 * (6 * t + j)
                    u_ref[at, 384 * t + 128 * j : 384 * t + 128 * j + 128] = bulk_ref[
                        8 * p + k, base : base + 32
                    ]
    for t in range(2):
        v_ref[:, 384 * t : 384 * t + 384] = dot(u_ref[:, 384 * t : 384 * t + 384], d_ref[t])
    c_ref[...] = -dot_nt(v_ref[...], u_ref[...])
    for p in range(2):
        for k in range(8):
            for j in range(2):
                at = (
                    slice(256 * p + 32 * k, 256 * p + 32 * k + 32),
                    slice(256 * p + 128 * j, 256 * p + 128 * j + 128),
                )
                c_ref[at] = c_ref[at] + early_ref[8 * p + k, 144 + 32 * j : 176 + 32 * j]

    def step(kb, carry):
        sweep_refs([c_ref], kb)
        return carry

    lax.fori_loop(0, 4, step, 0)
    blank = jnp.zeros((48, 256), jnp.float32)
    rows, direct = [], []
    for t in range(2):
        low, high = choose(upper, ei_ref[t], blank)
        placed = jnp.concatenate([low, high], 1)
        rows.append(placed - dot_nt(es_ref[t], v_ref[:, 384 * t : 384 * t + 384]))
        direct.append(dot(es_ref[t], d_ref[t]))
    none = jnp.zeros((48, 384), jnp.float32)
    g = -dot(jnp.concatenate(rows, 0), c_ref[...])
    t_s = (
        jnp.concatenate(
            [
                jnp.concatenate([direct[0], none], 1),
                jnp.concatenate([none, direct[1]], 1),
            ],
            0,
        )
        - dot(g, v_ref[...])
    )
    columns = []
    for p in range(2):
        for t in range(2):
            for k in range(8):
                for j in range(3):
                    base = 384 + 144 * t + 48 * j
                    l_ref[48 * k : 48 * k + 48, 128 * j : 128 * j + 128] = bulk_ref[
                        8 * p + k, base : base + 48
                    ]
                    base = 32 * (6 * t + 3 + j)
                    l_ref[384 + 32 * k : 416 + 32 * k, 128 * j : 128 * j + 128] = bulk_ref[
                        8 * p + k, base : base + 32
                    ]
            weights = jnp.concatenate(
                [t_s[:, 384 * t : 384 * t + 384], g[:, 256 * p : 256 * p + 256]], 1
            )
            own = jnp.where(where_ref[2] == p, lee_ref[t], 0.0)
            placed = jnp.concatenate([own, none] if t == 0 else [none, own], 0)
            columns.append(placed - dot(weights, l_ref[...]))
    out = jnp.concatenate(columns, 1)
    keep_ref[...], send_ref[...] = choose(first, out[0:48], out[48:96])


def call(kernel, outs, args, scratch=()):
    shapes = [jax.ShapeDtypeStruct(s, jnp.float32) for s in outs]
    specs = [pl.BlockSpec(memory_space=pltpu.SMEM)]
    specs += [pl.BlockSpec(memory_space=pltpu.VMEM) for _ in args[1:]]
    return pl.pallas_call(
        kernel,
        out_shape=shapes,
        in_specs=specs,
        out_specs=[pl.BlockSpec(memory_space=pltpu.VMEM) for _ in outs],
        scratch_shapes=[pltpu.VMEM(s, jnp.float32) for s in scratch],
        compiler_params=pltpu.CompilerParams(vmem_limit_bytes=VMEM_LIMIT),
    )(*args)


def swap(x, axis):
    return lax.ppermute(x, axis, [(0, 1), (1, 0)])


def by_slot(core, mine, other):
    first = core == 0
    return jnp.stack([jnp.where(first, mine, other), jnp.where(first, other, mine)])[:, None]


def local(interface_rows, exterior_rows, pml_mask):
    core = lax.axis_index("core")
    blk = lax.axis_index(("xl", "z"))
    where = jnp.stack([core, blk, lax.axis_index("xh")]).astype(jnp.int32)
    mine, send = call(
        damp_kernel,
        [(128, 1024), (128, 1024)],
        [where, interface_rows[:, 0], exterior_rows[:, 0], pml_mask],
    )
    recv = swap(send, "core")
    keep, away, s1, bulk, es, ei, lee = call(
        split_kernel,
        [
            (3, 48, 128),
            (3, 48, 128),
            (2, 32, 128),
            (672, 128),
            (2, 48, 384),
            (2, 48, 256),
            (2, 48, 384),
        ],
        [where, mine, recv],
    )
    bulk_all = lax.all_gather(bulk, PLANE, axis=0, tiled=False)
    shared = keep + swap(away, "xh")
    early = jnp.concatenate([shared.reshape(144, 128), s1.reshape(64, 128)], 0)
    early_all = lax.all_to_all(
        jnp.broadcast_to(early[None], (16, 208, 128)), PLANE, 0, 0, tiled=False
    )
    d_inv, s_inv = call(
        first_kernel,
        [(2, 384, 384), (256, 256)],
        [where, early_all],
        scratch=[(384, 384)] * 3,
    )
    one_keep, one_send = call(
        one_kernel,
        [(96, 1536), (96, 1536)],
        [where, bulk_all, s_inv, mine, recv],
        scratch=[(256, 1536)],
    )
    one_recv = swap(one_send, "core")
    two_keep, two_send = call(
        two_kernel,
        [(48, 1536), (48, 1536)],
        [where, bulk_all, early_all, d_inv, es, ei, lee],
        scratch=[(512, 768), (512, 768), (512, 512), (640, 384)],
    )
    two_recv = swap(two_send, "core")
    return by_slot(core, one_keep, one_recv), by_slot(core, two_keep, two_recv)


def solution(mesh):
    fine = Mesh(mesh.devices.reshape(4, 2, 2, 2, 4), ("y", "xh", "core", "xl", "z"))
    box, blk = ("y", "xh", "core"), ("xl", "z")
    rows = P(None, box, blk, None)
    return jax.shard_map(
        local,
        mesh=fine,
        in_specs=(rows, rows, P(None, box, None)),
        out_specs=(rows, rows),
        check_vma=False,
    )
```

time: 1010 us -> 149 us (0.15)
  other arithmetic: 518 us -> 2.17 us
  waiting for transfers between devices: 283 us -> 4.51 us
  local copies, waits for them, and re-layouts: 111 us -> 7.94 us
  Pallas kernels: 0 us -> 77.2 us
  matrix products: 63.7 us -> 0 us
  blocking collectives: 0 us -> 36.4 us
    another operation x41 -> x3, other arithmetic: 485 us -> 0.2 us  [the longest x2 0.13 us: by_slot(): jnp.stack([jnp.where(first, mine, other), jnp.where(first, other, mine)])]
    ppermute x3 -> x4, waiting for transfers between devices: 187 us -> 4.49 us  [swap(): return lax.ppermute(x, axis, [(0, 1), (1, 0)])]
    all_gather x2 -> x1, waiting for transfers between devices: 96.3 us -> 0.01 us  [local(): bulk_all = lax.all_gather(bulk, PLANE, axis=0, tiled=False)]
    pallas_call x0 -> x5, Pallas kernels: none -> 77.2 us  [call(): pl.pallas_call(kernel, out_shape=shapes, in_specs=specs, out_specs=[pl.Bl...]
    another operation x40 -> x0, local copies, waits for them, and re-layouts: 49 us -> none
    another operation x40 -> x0, matrix products: 45.8 us -> none  [the longest x12 23 us: schur_terms(): return (jnp.linalg.cholesky(schur), coupled)]
    all_to_all x0 -> x1, blocking collectives: none -> 36.4 us  [local(): lax.all_to_all(jnp.broadcast_to(early[None], (16, 208, 128)), PLANE, 0, 0...]
    slice x9 -> x0, local copies, waits for them, and re-layouts: 35.7 us -> none  [the longest x3 19.4 us: reorder(): shared = grouped[..., 0, :].reshape(lead + (width // 2,))]
  transfers between devices with their start and end apart: 5 -> 5, of which waited for: 5 -> 3; matrix products, arithmetic and copies ran while one was open for 3% -> 1% of each run, Pallas kernels for 0% -> 24%
where the time goes in v1:
time: 149 us; the launch traced here: 148 us
  Pallas kernels  77.2 us (52%)
  blocking collectives  36.4 us (24%)
  between operations  14.1 us (9%)
  local copies, waits for them, and re-layouts  7.94 us (5%)
  starting transfers between devices  6.06 us (4%)
  waiting for transfers between devices  4.51 us (3%)
  other arithmetic  2.17 us (1%)
    pallas_call x5, Pallas kernels, call(): pl.pallas_call(kernel, out_shape=shapes, in_specs=specs, out_specs=[pl.Bl...  77.2 us
    all_to_all x1, blocking collectives, local(): lax.all_to_all(jnp.broadcast_to(early[None], (16, 208, 128)), PLANE, 0, 0...  36.4 us
    unnamed x20, local copies, waits for them, and re-layouts  7.83 us
    ppermute x4, starting transfers between devices, swap(): return lax.ppermute(x, axis, [(0, 1), (1, 0)])  6.03 us
    ppermute x4, waiting for transfers between devices, swap(): return lax.ppermute(x, axis, [(0, 1), (1, 0)])  4.49 us
  transfers between devices with their start and end apart: 5, of which 3 were waited for; matrix products, arithmetic and copies ran while one was open for 1% of the time, Pallas kernels for 24%

profile of v1, /device:TPU:1, one launch (start us, length us, event | category | flops | bytes accessed | tf_op | source)
XLA Modules:
  0.0 148.4 jit_solution(7933301855914007262)
XLA Ops:
  7.2 0.0 all-gather.3.cloned.1.call-start
  7.2 0.1 pad_add_fusion.where_ref
  7.3 0.0 copy-start.6
  7.3 0.0 copy-start.2
  7.3 1.1 copy-done.2
  8.4 0.0 copy-start.3
  8.4 0.9 copy-done.3
  9.4 0.0 copy-start.9
  9.4 0.7 copy-done.9
  10.1 0.7 shard_map.50
  10.8 1.5 %collective-permute-start = (f32[128,1024]{1,0:T(8,128)S(1)}, f32[128,1024]{1,0:T(8,128)S(1)}, u32[]{:S(2)}, u32[]{:S(2)}) collective-permute-start(f32[128,1024]{1,0:T(8,128)S(1)} %get-tuple-element.18), channel_id=1, source_target_pairs={{0,8},{8,0},{1,9},{9,1},{2,10},{10,2},{3,11},{11,3},{4,12},{12,4},... | collective-permute-start | bytes 1572872 | tf_op jit(solution)/shard_map/ppermute | solution.py:368
  12.3 1.5 %collective-permute-done.recv_ref = f32[128,1024]{1,0:T(8,128)S(1)} collective-permute-done((f32[128,1024]{1,0:T(8,128)S(1)}, f32[128,1024]{1,0:T(8,128)S(1)}, u32[]{:S(2)}, u32[]{:S(2)}) %collective-permute-start) | collective-permute-done | bytes 524320 | tf_op jit(solution)/shard_map/ppermute | solution.py:368
  13.8 2.0 %shard_map.51 = (f32[3,48,128]{2,1,0:T(8,128)S(1)}, f32[3,48,128]{2,1,0:T(8,128)S(1)}, f32[2,32,128]{2,1,0:T(8,128)S(1)}, f32[672,128]{1,0:T(8,128)}, f32[2,48,3...) custom-call(s32[3]{0:T(128)S(1)} %pad_add_fusion.where_ref, ...), custom_call_target="tpu_custom_call" | custom-call | tf_op jit(solution)/shard_map/pallas_call | solution.py:357
  15.8 0.0 copy-start.4
  15.8 0.7 copy-done.4
  16.5 0.0 all-gather.3.cloned.1.call-update
  16.5 2.9 %collective-permute-start.1 = (f32[3,48,128]{2,1,0:T(8,128)S(1)}, f32[3,48,128]{2,1,0:T(8,128)S(1)}, u32[]{:S(2)}, u32[]{:S(2)}) collective-permute-start(f32[3,48,128]{2,1,0:T(8,128)S(1)} %get-tuple-element.21), channel_id=1, source_target_pairs={{0,16},{16,0},{1,17},{17,1},{2,18},{18,2},{3,19},{19,3},{4,20},{20... | collective-permute-start | bytes 221192 | tf_op jit(solution)/shard_map/ppermute | solution.py:368
  19.4 1.9 %collective-permute-done.1 = f32[3,48,128]{2,1,0:T(8,128)S(1)} collective-permute-done((f32[3,48,128]{2,1,0:T(8,128)S(1)}, f32[3,48,128]{2,1,0:T(8,128)S(1)}, u32[]{:S(2)}, u32[]{:S(2)}) %collective-permute-start.1) | collective-permute-done | bytes 73760 | tf_op jit(solution)/shard_map/ppermute | solution.py:368
  21.3 0.1 broadcast_in_dim.12
  21.5 36.4 %all_to_all.5.early_ref = f32[16,208,128]{2,1,0:T(8,128)S(1)} all-to-all(f32[16,208,128]{2,1,0:T(8,128)S(1)} %broadcast_in_dim.12), channel_id=1, replica_groups=mesh['y'=4,'xh'=2,'core'=2,'xl'=2,'z'=4] {'xh','xl','z'}, dimensions={0} | all-to-all | bytes 3407872 | tf_op jit(solution)/shard_map/all_to_all | solution.py:402
  57.9 0.0 copy-done.6
  57.9 31.8 %shard_map.52 = (f32[2,384,384]{2,1,0:T(8,128)S(1)}, f32[256,256]{1,0:T(8,128)S(1)}) custom-call(s32[3]{0:T(128)S(1)} %pad_add_fusion.where_ref, f32[16,208,128]{2,1,0:T(8,128)S(1)} %all_to_all.5.early_ref), custom_call_target="tpu_custom_call" | custom-call | tf_op jit(solution)/shard_map/pallas_call | solution.py:357
  89.7 0.0 copy-start
  89.7 1.0 copy-done
  90.7 0.0 all-gather.3.cloned.1.call-done
  90.7 0.0 copy-start.1
  90.7 1.3 copy-done.1
  92.0 0.0 copy-start.5
  92.0 0.9 copy-done.5
  92.9 0.0 copy-start.7
  92.9 0.6 copy-done.7
  93.5 38.3 %shard_map.54 = (f32[48,1536]{1,0:T(8,128)S(1)}, f32[48,1536]{1,0:T(8,128)}) custom-call(s32[3]{0:T(128)S(1)} %copy-done.7, f32[16,672,128]{2,1,0:T(8,128)} %bitcast.27, f32[16,208,128]{2,1,0:T(8,128)S(1)} %all_to_all.5.early_ref, f32[2,384,384]{2,1,0:T(8,128)S(1)} %copy-done.1, f32[2,48,384]{2,1,0:T(8,128)S(1)} %get-tuple-element.27.es_ref, ...), custom_call_target="tpu_custom_call" | custom-call | tf_op jit(solution)/shard_map/pallas_call | solution.py:357
  131.8 1.5 %collective-permute-start.3 = (f32[48,1536]{1,0:T(8,128)}, f32[48,1536]{1,0:T(8,128)S(1)}, u32[]{:S(2)}, u32[]{:S(2)}) collective-permute-start(f32[48,1536]{1,0:T(8,128)} %get-tuple-element.31), channel_id=1, source_target_pairs={{0,8},{8,0},{1,9},{9,1},{2,10},{10,2},{3,11},{11,3},{4,12},{12,4},... | collective-permute-start | bytes 884744 | tf_op jit(solution)/shard_map/ppermute | solution.py:368
  133.4 0.0 copy-start.8
  133.4 0.6 copy-done.8
  133.9 4.3 %shard_map.53 = (f32[96,1536]{1,0:T(8,128)S(1)}, f32[96,1536]{1,0:T(8,128)S(1)}) custom-call(s32[3]{0:T(128)S(1)} %copy-done.8, f32[16,672,128]{2,1,0:T(8,128)} %bitcast.28, f32[256,256]{1,0:T(8,128)S(1)} %get-tuple-element.23.s_ref, f32[128,1024]{1,0:T(8,128)S(1)} %get-tuple-element.17.mine_ref, f32[128,1024]{1,0:T(8,128)S(1)} %collective-permute-done.recv_ref), custom_call_target="tpu_custom_call" | custom-call | tf_op jit(solution)/shard_map/pallas_call | solution.py:357
  138.3 0.1 collective-permute-start.2
  138.4 0.0 collective-permute-done.3
  138.4 0.9 maximum_bitcast_fusion.1
  139.3 1.1 collective-permute-done.2
  140.4 0.1 select_bitcast_fusion.1
  140.4 1.1 maximum_bitcast_fusion
  (3 shorter events, 0.1 us)
Async XLA Ops:
  7.2 83.5 %all-gather.3.cloned.1.call-start = ((), (), s32[]{:S(2)}) async-start(), calls=%async_computation.1 | async-start | bytes 5849088 | tf_op jit(solution)/shard_map/all_gather | solution.py:399
  7.3 50.6 %copy-start.6 = (s32[3]{0:T(128)}, s32[3]{0:T(128)S(1)}, u32[]{:S(2)}) copy-start(s32[3]{0:T(128)S(1)} %pad_add_fusion.where_ref) | copy-start | bytes 40
  7.3 1.1 copy-start.2
  8.4 0.9 copy-start.3
  9.4 0.7 copy-start.9
  10.8 3.0 %collective-permute-start = (f32[128,1024]{1,0:T(8,128)S(1)}, f32[128,1024]{1,0:T(8,128)S(1)}, u32[]{:S(2)}, u32[]{:S(2)}) collective-permute-start(f32[128,1024]{1,0:T(8,128)S(1)} %get-tuple-element.18), channel_id=1, source_target_pairs={{0,8},{8,0},{1,9},{9,1},{2,10},{10,2},{3,11},{11,3},{4,12},{12,4},... | collective-permute-start | bytes 1572872 | tf_op jit(solution)/shard_map/ppermute | solution.py:368
  15.8 0.7 copy-start.4
  16.5 4.8 %collective-permute-start.1 = (f32[3,48,128]{2,1,0:T(8,128)S(1)}, f32[3,48,128]{2,1,0:T(8,128)S(1)}, u32[]{:S(2)}, u32[]{:S(2)}) collective-permute-start(f32[3,48,128]{2,1,0:T(8,128)S(1)} %get-tuple-element.21), channel_id=1, source_target_pairs={{0,16},{16,0},{1,17},{17,1},{2,18},{18,2},{3,19},{19,3},{4,20},{20... | collective-permute-start | bytes 221192 | tf_op jit(solution)/shard_map/ppermute | solution.py:368
  89.7 1.0 copy-start
  90.7 1.3 copy-start.1
  92.0 0.9 copy-start.5
  92.9 0.6 copy-start.7
  131.8 6.5 %collective-permute-start.3 = (f32[48,1536]{1,0:T(8,128)}, f32[48,1536]{1,0:T(8,128)S(1)}, u32[]{:S(2)}, u32[]{:S(2)}) collective-permute-start(f32[48,1536]{1,0:T(8,128)} %get-tuple-element.31), channel_id=1, source_target_pairs={{0,8},{8,0},{1,9},{9,1},{2,10},{10,2},{3,11},{11,3},{4,12},{12,4},... | collective-permute-start | bytes 884744 | tf_op jit(solution)/shard_map/ppermute | solution.py:368
  133.4 0.6 copy-start.8
  138.3 2.1 %collective-permute-start.2 = (f32[96,1536]{1,0:T(8,128)S(1)}, f32[96,1536]{1,0:T(8,128)S(1)}, u32[]{:S(2)}, u32[]{:S(2)}) collective-permute-start(f32[96,1536]{1,0:T(8,128)S(1)} %get-tuple-element.25), channel_id=1, source_target_pairs={{0,8},{8,0},{1,9},{9,1},{2,10},{10,2},{3,11},{11,3},{4,12},{12,4},... | collective-permute-start | bytes 1769480 | tf_op jit(solution)/shard_map/ppermute | solution.py:368
Sparse Core Ops, SparseCore 0:
  16.6 73.6 all-gather.2

commit v2 on v1

--- a/solution.py
+++ b/solution.py
@@ -10,7 +10,6 @@
 
 HI = lax.Precision.HIGHEST
 DAMPING = 2.0
-VMEM_LIMIT = 48 * 2**20
 PLANE = ("xh", "xl", "z")
 
 
@@ -24,27 +23,7 @@
     )
 
 
-def small_sweep(entries):
-    n = len(entries)
-    a = [[entries[max(i, j)][min(i, j)] for j in range(n)] for i in range(n)]
-    for k in range(n):
-        r = 1.0 / a[k][k]
-        u = [a[k][j] * r for j in range(n)]
-        new = [[None] * n for _ in range(n)]
-        for i in range(n):
-            for j in range(i + 1):
-                if i == k and j == k:
-                    v = -r
-                elif i == k:
-                    v = u[j]
-                elif j == k:
-                    v = u[i]
-                else:
-                    v = a[i][j] - a[i][k] * u[j]
-                new[i][j] = v
-                new[j][i] = v
-        a = new
-    return a
+PANEL = 16
 
 
 def tree_sum(t):
@@ -53,61 +32,72 @@
     return t[0]
 
 
-def pivot_rows(row, k, lane):
-    w = row.shape[1]
-    inblk = (lane >= 8 * k) & (lane < 8 * k + 8)
-    col = [jnp.broadcast_to(row[:, 8 * k + q : 8 * k + q + 1], (8, w)) for q in range(8)]
-    entries = [
-        [jnp.broadcast_to(col[j][i : i + 1], (8, w)) if j <= i else None for j in range(8)]
-        for i in range(8)
+def spread_lane(x, at):
+    return jnp.broadcast_to(x[:, at : at + 1], x.shape)
+
+
+def spread_row(x, at):
+    return jnp.broadcast_to(x[at : at + 1], x.shape)
+
+
+def eliminate(rows, base, lane, sub):
+    count = 8 * len(rows)
+    cols = [[spread_lane(x, base + q) for x in rows] for q in range(count)]
+    inblk = (lane >= base) & (lane < base + count)
+    out = [
+        jnp.where(inblk, jnp.where(lane == sub + (8 * v + base), -1.0, 0.0), x)
+        for v, x in enumerate(rows)
     ]
-    m = small_sweep(entries)
-    rb = [
-        jnp.where(
-            inblk,
-            jnp.where(lane == 8 * k + j, -1.0, 0.0),
-            jnp.broadcast_to(row[j : j + 1], (8, w)),
-        )
-        for j in range(8)
-    ]
-    return [tree_sum([m[i][j] * rb[j] for j in range(8)]) for i in range(8)]
+    for k in range(count):
+        kv, ks = divmod(k, 8)
+        scale = 1.0 / spread_row(cols[k][kv], ks)
+        hit = sub == ks
+
+        def update(tiles):
+            row = spread_row(tiles[kv], ks) * scale
+            new = [x - c * row for x, c in zip(tiles, cols[k])]
+            new[kv] = jnp.where(hit, row, new[kv])
+            return new
+
+        for j in range(k + 1, count):
+            cols[j] = update(cols[j])
+        out = update(out)
+    return out
 
 
 def sweep_blocks(mats):
-    n = 128
-    steps = n // 8
-    lane = lax.broadcasted_iota(jnp.int32, (8, n), 1)
-    sub = lax.broadcasted_iota(jnp.int32, (8, n), 0)
-    full_lane = lax.broadcasted_iota(jnp.int32, (n, n), 1)
-    mats = list(mats)
-    rows = [a[0:8] for a in mats]
-    for k in range(steps):
-        inblk = (lane >= 8 * k) & (lane < 8 * k + 8)
-        full_in = (full_lane >= 8 * k) & (full_lane < 8 * k + 8)
-        next_mats, next_rows = [], []
-        for a, row in zip(mats, rows):
-            news = pivot_rows(row, k, lane)
-            packed = news[7]
-            for i in range(7):
-                packed = jnp.where(sub == i, news[i], packed)
-            if k < steps - 1:
-                ahead = a[8 * k + 8 : 8 * k + 16]
-                terms = [
-                    jnp.broadcast_to(ahead[:, 8 * k + q : 8 * k + q + 1], (8, n)) * news[q]
-                    for q in range(8)
-                ]
-                next_rows.append(jnp.where(inblk, 0.0, ahead) + tree_sum(terms))
-            zero = jnp.zeros((8, n), jnp.float32)
-            spread = jnp.concatenate([packed if v == k else zero for v in range(steps)], 0)
-            full = jnp.where(full_in, 0.0, a) + dot(jnp.where(full_in, a, 0.0), spread)
-            parts = ([full[: 8 * k]] if k > 0 else []) + [-packed]
-            if k < steps - 1:
-                parts.append(next_rows[-1])
-                if k < steps - 2:
-                    parts.append(full[8 * k + 16 :])
-            next_mats.append(jnp.concatenate(parts, 0))
-        mats, rows = next_mats, next_rows
-    return mats
+    tiles, per = 16, PANEL // 8
+    lane = lax.broadcasted_iota(jnp.int32, (8, 128), 1)
+    sub = lax.broadcasted_iota(jnp.int32, (8, 128), 0)
+    mats = [[a[8 * i : 8 * i + 8] for i in range(tiles)] for a in mats]
+    for k in range(tiles // per):
+        base = PANEL * k
+        inblk = (lane >= base) & (lane < base + PANEL)
+        own = range(per * k, per * k + per)
+        near = range(per * k + per, min(per * k + 2 * per, tiles))
+        for c, rows in enumerate(mats):
+            cols = {t: [spread_lane(rows[t], base + q) for q in range(PANEL)] for t in near}
+            solved = eliminate([rows[t] for t in own], base, lane, sub)
+            new = list(rows)
+            if near:
+                each = [spread_row(solved[q // 8], q % 8) for q in range(PANEL)]
+                for t in near:
+                    total = tree_sum([cols[t][q] * each[q] for q in range(PANEL)])
+                    new[t] = jnp.where(inblk, 0.0, rows[t]) - total
+            change = lax.dot_general(
+                jnp.concatenate([rows[t] for t in own], 0),
+                jnp.concatenate(solved, 0),
+                (((0,), (0,)), ((), ())),
+                precision=HI,
+                preferred_element_type=jnp.float32,
+            )
+            for t in range(tiles):
+                if t in own:
+                    new[t] = solved[t - per * k]
+                elif t not in near:
+                    new[t] = jnp.where(inblk, 0.0, rows[t]) - change[8 * t : 8 * t + 8]
+            mats[c] = new
+    return [jnp.concatenate(rows, 0) for rows in mats]
 
 
 def sweep_refs(refs, kb):
@@ -173,10 +163,22 @@
     return jnp.where(first, a, b), jnp.where(first, b, a)
 
 
-def damp_kernel(where_ref, inner_ref, outer_ref, mask_ref, mine_ref, send_ref):
+def damp_kernel(
+    where_ref, inner_hbm, outer_hbm, mask_hbm, mine_ref, send_ref, inner_ref, outer_ref, mask_ref, sems
+):
+    copies = [
+        pltpu.make_async_copy(a, b, sems.at[i])
+        for i, (a, b) in enumerate(
+            ((mask_hbm, mask_ref), (inner_hbm, inner_ref), (outer_hbm, outer_ref))
+        )
+    ]
+    for copy in copies:
+        copy.start()
+    for copy in copies:
+        copy.wait()
     core, blk = where_ref[0], where_ref[1]
     for out_ref, slot in ((mine_ref, core), (send_ref, 1 - core)):
-        gain = DAMPING * mask_ref[slot].astype(jnp.float32)
+        gain = DAMPING * mask_ref[slot, 0].astype(jnp.float32)
         for source, start, count, offset in (
             (inner_ref, 0, 32, blk * 32),
             (outer_ref, 32, 96, 256 + blk * 96),
@@ -184,7 +186,7 @@
             row = lax.broadcasted_iota(jnp.int32, (count, 1024), 0) + offset
             lane = lax.broadcasted_iota(jnp.int32, (count, 1024), 1)
             match = jnp.where(row == lane, 1.0, 0.0)
-            out_ref[start : start + count, :] = source[slot] + match * gain
+            out_ref[start : start + count, :] = source[slot, 0] + match * gain
 
 
 def split_kernel(
@@ -212,42 +214,55 @@
         keep_ref[j], send_ref[j] = choose(upper, kept[0][j], kept[1][j])
 
 
-def first_kernel(where_ref, early_ref, d_ref, s_ref, a_ref, b_ref, c_ref):
-    pair = where_ref[2]
-    row = lax.broadcasted_iota(jnp.int32, (384, 384), 0)
-    lane = lax.broadcasted_iota(jnp.int32, (384, 384), 1)
-    c_ref[...] = jnp.where(row == lane, 1.0, 0.0)
+def first_kernel(early_ref, d_ref):
     for k in range(8):
         for j in range(3):
             at = (slice(48 * k, 48 * k + 48), slice(128 * j, 128 * j + 128))
-            a_ref[at] = early_ref[k, 48 * j : 48 * j + 48]
-            b_ref[at] = early_ref[8 + k, 48 * j : 48 * j + 48]
+            for t in range(2):
+                d_ref[(t,) + at] = early_ref[8 * t + k, 48 * j : 48 * j + 48]
+
+    def step(kb, carry):
+        sweep_refs([d_ref.at[0], d_ref.at[1]], kb)
+        return carry
+
+    lax.fori_loop(0, 3, step, 0)
+    d_ref[...] = -d_ref[...]
+
+
+def inner_kernel(s1_ref, out_ref):
+    for k in range(8):
         for j in range(2):
-            c_ref[32 * k : 32 * k + 32, 128 * j : 128 * j + 128] = early_ref[
-                8 * pair + k, 144 + 32 * j : 176 + 32 * j
-            ]
+            out_ref[32 * k : 32 * k + 32, 128 * j : 128 * j + 128] = s1_ref[k, j]
 
     def step(kb, carry):
-        sweep_refs([a_ref, b_ref, c_ref], kb)
+        sweep_refs([out_ref], kb)
         return carry
 
-    lax.fori_loop(0, 3, step, 0)
-    d_ref[0] = -a_ref[...]
-    d_ref[1] = -b_ref[...]
-    s_ref[...] = -c_ref[0:256, 0:256]
-
-
-def one_kernel(where_ref, bulk_ref, s_ref, mine_ref, recv_ref, keep_ref, send_ref, u_ref):
+    lax.fori_loop(0, 2, step, 0)
+    out_ref[...] = -out_ref[...]
+
+
+def one_kernel(
+    where_ref, bulk_hbm, s_ref, mine_ref, recv_ref, keep_ref, send_ref, bulk_ref, u_ref, sems
+):
     first = where_ref[0] == 0
     pair = where_ref[2]
-    for k in range(8):
+    copies = [
+        pltpu.make_async_copy(bulk_hbm.at[8 * pair + k, 0:384], bulk_ref.at[k], sems.at[k])
+        for k in range(8)
+    ]
+    for copy in copies:
+        copy.start()
+    boxes = choose(first, mine_ref[32:128, :], recv_ref[32:128, :])
+    left = jnp.concatenate([boxes[0][:, 0:256], boxes[1][:, 0:256]], 0)
+    left = dot(left, s_ref[...])
+    for k, copy in enumerate(copies):
+        copy.wait()
         for j in range(12):
             u_ref[32 * k : 32 * k + 32, 128 * j : 128 * j + 128] = bulk_ref[
-                8 * pair + k, 32 * j : 32 * j + 32
+                k, 32 * j : 32 * j + 32
             ]
-    boxes = choose(first, mine_ref[32:128, :], recv_ref[32:128, :])
-    left = jnp.concatenate([boxes[0][:, 0:256], boxes[1][:, 0:256]], 0)
-    right = dot(dot(left, s_ref[...]), u_ref[...])
+    right = dot(left, u_ref[...])
     outs = []
     for t in range(2):
         block = right[96 * t : 96 * t + 96]
@@ -267,8 +282,9 @@
 
 def two_kernel(
     where_ref,
-    bulk_ref,
-    early_ref,
+    bulk_hbm,
+    s1_ref,
+    s1_far_ref,
     d_ref,
     es_ref,
     ei_ref,
@@ -279,9 +295,26 @@
     v_ref,
     c_ref,
     l_ref,
+    bulk_ref,
+    sems,
 ):
     first = where_ref[0] == 0
     upper = where_ref[2] == 0
+    parts = (slice(0, 384), slice(384, 672))
+    copies = [
+        [
+            pltpu.make_async_copy(
+                bulk_hbm.at[i, part], bulk_ref.at[i, part], sems.at[16 * h + i]
+            )
+            for i in range(16)
+        ]
+        for h, part in enumerate(parts)
+    ]
+    for group in copies:
+        for copy in group:
+            copy.start()
+    for copy in copies[0]:
+        copy.wait()
     for p in range(2):
         for k in range(8):
             at = slice(256 * p + 32 * k, 256 * p + 32 * k + 32)
@@ -294,14 +327,14 @@
     for t in range(2):
         v_ref[:, 384 * t : 384 * t + 384] = dot(u_ref[:, 384 * t : 384 * t + 384], d_ref[t])
     c_ref[...] = -dot_nt(v_ref[...], u_ref[...])
-    for p in range(2):
-        for k in range(8):
-            for j in range(2):
+    for k in range(8):
+        for j in range(2):
+            for p, block in enumerate(choose(upper, s1_ref[k, j], s1_far_ref[k, j])):
                 at = (
                     slice(256 * p + 32 * k, 256 * p + 32 * k + 32),
                     slice(256 * p + 128 * j, 256 * p + 128 * j + 128),
                 )
-                c_ref[at] = c_ref[at] + early_ref[8 * p + k, 144 + 32 * j : 176 + 32 * j]
+                c_ref[at] = c_ref[at] + block
 
     def step(kb, carry):
         sweep_refs([c_ref], kb)
@@ -327,6 +360,8 @@
         )
         - dot(g, v_ref[...])
     )
+    for copy in copies[1]:
+        copy.wait()
     columns = []
     for p in range(2):
         for t in range(2):
@@ -350,27 +385,51 @@
     keep_ref[...], send_ref[...] = choose(first, out[0:48], out[48:96])
 
 
-def call(kernel, outs, args, scratch=()):
+def call(kernel, outs, args, micros, limit, scratch=(), scalars=True, hbm=0):
     shapes = [jax.ShapeDtypeStruct(s, jnp.float32) for s in outs]
-    specs = [pl.BlockSpec(memory_space=pltpu.SMEM)]
-    specs += [pl.BlockSpec(memory_space=pltpu.VMEM) for _ in args[1:]]
+    specs = [pl.BlockSpec(memory_space=pltpu.SMEM)] if scalars else []
+    specs += [pl.BlockSpec(memory_space=pltpu.HBM)] * hbm
+    specs += [pl.BlockSpec(memory_space=pltpu.VMEM)] * (len(args) - len(specs))
     return pl.pallas_call(
         kernel,
         out_shape=shapes,
         in_specs=specs,
         out_specs=[pl.BlockSpec(memory_space=pltpu.VMEM) for _ in outs],
-        scratch_shapes=[pltpu.VMEM(s, jnp.float32) for s in scratch],
-        compiler_params=pltpu.CompilerParams(vmem_limit_bytes=VMEM_LIMIT),
+        scratch_shapes=scratch,
+        compiler_params=pltpu.CompilerParams(vmem_limit_bytes=limit * 2**20),
+        cost_estimate=pl.CostEstimate(
+            flops=int(micros * 1e9), bytes_accessed=2**20, transcendentals=0
+        ),
     )(*args)
 
 
 def swap(x, axis):
     return lax.ppermute(x, axis, [(0, 1), (1, 0)])
+
+
+def ring_gather(x):
+    z = lax.axis_index("z")
+    parts = [x] + [lax.ppermute(x, "z", [(i, (i + d) % 4) for i in range(4)]) for d in (1, 2, 3)]
+    ordered = []
+    for owner in range(4):
+        step = (z - owner) % 4
+        ordered.append(
+            jnp.where(
+                step < 2,
+                jnp.where(step == 0, parts[0], parts[1]),
+                jnp.where(step == 2, parts[2], parts[3]),
+            )
+        )
+    return jnp.stack(ordered)
 
 
 def by_slot(core, mine, other):
     first = core == 0
     return jnp.stack([jnp.where(first, mine, other), jnp.where(first, other, mine)])[:, None]
+
+
+def floats(*shape):
+    return pltpu.VMEM(shape, jnp.float32)
 
 
 def local(interface_rows, exterior_rows, pml_mask):
@@ -380,7 +439,16 @@
     mine, send = call(
         damp_kernel,
         [(128, 1024), (128, 1024)],
-        [where, interface_rows[:, 0], exterior_rows[:, 0], pml_mask],
+        [where, interface_rows, exterior_rows, pml_mask],
+        1,
+        8,
+        hbm=3,
+        scratch=[
+            floats(2, 1, 32, 1024),
+            floats(2, 1, 96, 1024),
+            pltpu.VMEM((2, 1, 1024), jnp.int32),
+            pltpu.SemaphoreType.DMA((3,)),
+        ],
     )
     recv = swap(send, "core")
     keep, away, s1, bulk, es, ei, lee = call(
@@ -395,31 +463,51 @@
             (2, 48, 384),
         ],
         [where, mine, recv],
+        2,
+        8,
     )
     bulk_all = lax.all_gather(bulk, PLANE, axis=0, tiled=False)
     shared = keep + swap(away, "xh")
-    early = jnp.concatenate([shared.reshape(144, 128), s1.reshape(64, 128)], 0)
+    near = ring_gather(s1)
     early_all = lax.all_to_all(
-        jnp.broadcast_to(early[None], (16, 208, 128)), PLANE, 0, 0, tiled=False
-    )
-    d_inv, s_inv = call(
-        first_kernel,
-        [(2, 384, 384), (256, 256)],
-        [where, early_all],
-        scratch=[(384, 384)] * 3,
-    )
+        jnp.broadcast_to(shared.reshape(144, 128), (16, 144, 128)), PLANE, 0, 0, tiled=False
+    )
+    near, early_all = lax.optimization_barrier((near, early_all))
+    across = swap(near, "xl")
+    (d_inv,) = call(first_kernel, [(2, 384, 384)], [early_all], 17, 12, scalars=False)
+    low = lax.axis_index("xl") == 0
+    s1_own = jnp.concatenate(
+        [jnp.where(low, near, across), jnp.where(low, across, near)], 0
+    )
+    s1_own, d_inv = lax.optimization_barrier((s1_own, d_inv))
+    s1_far = swap(s1_own, "xh")
+    (s_inv,) = call(inner_kernel, [(256, 256)], [s1_own], 8, 8, scalars=False)
     one_keep, one_send = call(
         one_kernel,
         [(96, 1536), (96, 1536)],
         [where, bulk_all, s_inv, mine, recv],
-        scratch=[(256, 1536)],
+        3,
+        12,
+        hbm=1,
+        scratch=[floats(8, 384, 128), floats(256, 1536), pltpu.SemaphoreType.DMA((8,))],
     )
     one_recv = swap(one_send, "core")
+    bulk_late, one_keep = lax.optimization_barrier((bulk_all, one_keep))
     two_keep, two_send = call(
         two_kernel,
         [(48, 1536), (48, 1536)],
-        [where, bulk_all, early_all, d_inv, es, ei, lee],
-        scratch=[(512, 768), (512, 768), (512, 512), (640, 384)],
+        [where, bulk_late, s1_own, s1_far, d_inv, es, ei, lee],
+        25,
+        24,
+        hbm=1,
+        scratch=[
+            floats(512, 768),
+            floats(512, 768),
+            floats(512, 512),
+            floats(640, 384),
+            floats(16, 672, 128),
+            pltpu.SemaphoreType.DMA((32,)),
+        ],
     )
     two_recv = swap(two_send, "core")
     return by_slot(core, one_keep, one_recv), by_slot(core, two_keep, two_recv)

time: 149 us -> 148 us (level)
  blocking collectives: 36.4 us -> 0 us
  waiting for transfers between devices: 4.51 us -> 28.1 us
  starting transfers between devices: 6.06 us -> 20 us
  Pallas kernels: 77.2 us -> 75.3 us
    all_to_all x1 -> x0, blocking collectives: 36.4 us -> none  [local(): lax.all_to_all(jnp.broadcast_to(early[None], (16, 208, 128)), PLANE, 0, 0...]
    all_to_all x0 -> x1, waiting for transfers between devices: none -> 9.82 us  [local(): lax.all_to_all(jnp.broadcast_to(shared.reshape(144, 128), (16, 144, 128))...]
    ppermute x0 -> x3, waiting for transfers between devices: none -> 8.02 us  [ring_gather(): lax.ppermute(x, 'z', [(i, (i + d) % 4) for i in range(4)])]
    all_to_all x0 -> x1, starting transfers between devices: none -> 7.68 us  [local(): lax.all_to_all(jnp.broadcast_to(shared.reshape(144, 128), (16, 144, 128))...]
    all_gather x1, waiting for transfers between devices: 0.01 us -> 5.74 us  [local(): bulk_all = lax.all_gather(bulk, PLANE, axis=0, tiled=False)]
    ppermute x0 -> x3, starting transfers between devices: none -> 3.73 us  [ring_gather(): lax.ppermute(x, 'z', [(i, (i + d) % 4) for i in range(4)])]
    ppermute x4 -> x6, starting transfers between devices: 6.03 us -> 8.51 us  [swap(): return lax.ppermute(x, axis, [(0, 1), (1, 0)])]
    pallas_call x5 -> x6, Pallas kernels: 77.2 us -> 75.3 us  [call(): pl.pallas_call(kernel, out_shape=shapes, in_specs=specs, out_specs=[pl.Bl...]
  transfers between devices with their start and end apart: 5 -> 11, of which waited for: 3 -> 8; matrix products, arithmetic and copies ran while one was open for 1% -> 1% of each run, Pallas kernels for 24% -> 23%
where the time goes in v2:
time: 148 us; the launch traced here: 147 us
  Pallas kernels  75.3 us (51%)
  waiting for transfers between devices  28.1 us (19%)
  starting transfers between devices  20 us (14%)
  between operations  14.2 us (10%)
  local copies, waits for them, and re-layouts  7.45 us (5%)
  other arithmetic  2.24 us (2%)
    pallas_call x6, Pallas kernels, call(): pl.pallas_call(kernel, out_shape=shapes, in_specs=specs, out_specs=[pl.Bl...  75.3 us
    all_to_all x1, waiting for transfers between devices, local(): lax.all_to_all(jnp.broadcast_to(shared.reshape(144, 128), (16, 144, 128))...  9.82 us
    ppermute x6, starting transfers between devices, swap(): return lax.ppermute(x, axis, [(0, 1), (1, 0)])  8.51 us
    ppermute x3, waiting for transfers between devices, ring_gather(): lax.ppermute(x, 'z', [(i, (i + d) % 4) for i in range(4)])  8.02 us
    all_to_all x1, starting transfers between devices, local(): lax.all_to_all(jnp.broadcast_to(shared.reshape(144, 128), (16, 144, 128))...  7.68 us
    unnamed x14, local copies, waits for them, and re-layouts  6.36 us
    all_gather x1, waiting for transfers between devices, local(): bulk_all = lax.all_gather(bulk, PLANE, axis=0, tiled=False)  5.74 us
    ppermute x6, waiting for transfers between devices, swap(): return lax.ppermute(x, axis, [(0, 1), (1, 0)])  4.54 us
  transfers between devices with their start and end apart: 11, of which 8 were waited for; matrix products, arithmetic and copies ran while one was open for 1% of the time, Pallas kernels for 23%

profile of v2, /device:TPU:1, one launch (start us, length us, event | category | flops | bytes accessed | tf_op | source)
XLA Modules:
  0.0 147.2 jit_solution(4638295142336385977)
XLA Ops:
  7.2 0.0 all-gather.3.cloned.1.call-start
  7.2 0.1 pad_add_fusion.where_ref
  7.3 0.0 copy-start.2
  7.3 1.1 copy-done.2
  8.4 0.0 copy-start.3
  8.4 0.9 copy-done.3
  9.4 0.0 copy-start.4
  9.4 0.7 copy-done.4
  10.1 0.8 shard_map.50
  10.9 1.5 %collective-permute-start = (f32[128,1024]{1,0:T(8,128)S(1)}, f32[128,1024]{1,0:T(8,128)S(1)}, u32[]{:S(2)}, u32[]{:S(2)}) collective-permute-start(f32[128,1024]{1,0:T(8,128)S(1)} %get-tuple-element.22), channel_id=1, source_target_pairs={{0,8},{8,0},{1,9},{9,1},{2,10},{10,2},{3,11},{11,3},{4,12},{12,4},... | collective-permute-start | bytes 1572872 | tf_op jit(solution)/shard_map/ppermute | solution.py:407
  12.4 1.5 %collective-permute-done.recv_ref = f32[128,1024]{1,0:T(8,128)S(1)} collective-permute-done((f32[128,1024]{1,0:T(8,128)S(1)}, f32[128,1024]{1,0:T(8,128)S(1)}, u32[]{:S(2)}, u32[]{:S(2)}) %collective-permute-start) | collective-permute-done | bytes 524320 | tf_op jit(solution)/shard_map/ppermute | solution.py:407
  13.9 2.0 %shard_map.51 = (f32[3,48,128]{2,1,0:T(8,128)S(1)}, f32[3,48,128]{2,1,0:T(8,128)S(1)}, f32[2,32,128]{2,1,0:T(8,128)S(1)}, f32[672,128]{1,0:T(8,128)}, f32[2,48,3...) custom-call(s32[3]{0:T(128)S(1)} %pad_add_fusion.where_ref, ...), custom_call_target="tpu_custom_call" | custom-call | flops 2000000000 | bytes 1048576 | tf_op jit(solution)/shard_map/pallas_call | solution.py:393
  16.0 0.0 all-gather.3.cloned.1.call-update
  16.0 2.9 %collective-permute-start.4 = (f32[3,48,128]{2,1,0:T(8,128)S(1)}, f32[3,48,128]{2,1,0:T(8,128)S(1)}, u32[]{:S(2)}, u32[]{:S(2)}) collective-permute-start(f32[3,48,128]{2,1,0:T(8,128)S(1)} %get-tuple-element.26), channel_id=1, source_target_pairs={{0,16},{16,0},{1,17},{17,1},{2,18},{18,2},{3,19},{19,3},{4,20},{20... | collective-permute-start | bytes 221192 | tf_op jit(solution)/shard_map/ppermute | solution.py:407
  18.9 1.9 %collective-permute-done.4 = f32[3,48,128]{2,1,0:T(8,128)S(1)} collective-permute-done((f32[3,48,128]{2,1,0:T(8,128)S(1)}, f32[3,48,128]{2,1,0:T(8,128)S(1)}, u32[]{:S(2)}, u32[]{:S(2)}) %collective-permute-start.4) | collective-permute-done | bytes 73760 | tf_op jit(solution)/shard_map/ppermute | solution.py:407
  20.8 1.1 broadcast_in_dim.9
  21.9 7.7 %all-to-all-start = ((f32[16,144,128]{2,1,0:T(8,128)}), f32[16,144,128]{2,1,0:T(8,128)S(1)}, u32[]{:S(2)}, u32[]{:S(2)}) async-start(f32[16,144,128]{2,1,0:T(8,128)} %broadcast_in_dim.9), calls=%async_computation | async-start | bytes 2359296 | tf_op jit(solution)/shard_map/all_to_all | solution.py:472
  29.6 2.6 %collective-permute-start.3 = (f32[2,32,128]{2,1,0:T(8,128)S(1)}, f32[2,32,128]{2,1,0:T(8,128)S(1)}, u32[]{:S(2)}, u32[]{:S(2)}) collective-permute-start(f32[2,32,128]{2,1,0:T(8,128)S(1)} %get-tuple-element.24), channel_id=1, source_target_pairs={{0,3},{1,0},{2,1},{3,2},{4,7},{5,4},{6,5},{7,6},{8,11},{9,8},{10,9... | collective-permute-start | bytes 98312 | tf_op jit(solution)/shard_map/ppermute | solution.py:412
  32.1 0.6 collective-permute-start.2
  32.7 0.6 collective-permute-start.1
  33.3 3.0 %collective-permute-done.3 = f32[2,32,128]{2,1,0:T(8,128)S(1)} collective-permute-done((f32[2,32,128]{2,1,0:T(8,128)S(1)}, f32[2,32,128]{2,1,0:T(8,128)S(1)}, u32[]{:S(2)}, u32[]{:S(2)}) %collective-permute-start.3) | collective-permute-done | bytes 32800 | tf_op jit(solution)/shard_map/ppermute | solution.py:412
  36.3 1.4 collective-permute-done.2
  37.7 3.6 %collective-permute-done.1 = f32[2,32,128]{2,1,0:T(8,128)S(1)} collective-permute-done((f32[2,32,128]{2,1,0:T(8,128)S(1)}, f32[2,32,128]{2,1,0:T(8,128)S(1)}, u32[]{:S(2)}, u32[]{:S(2)}) %collective-permute-start.1) | collective-permute-done | bytes 32800 | tf_op jit(solution)/shard_map/ppermute | solution.py:412
  41.4 9.8 %all-to-all-done.early_ref = f32[16,144,128]{2,1,0:T(8,128)S(1)} async-done(((f32[16,144,128]{2,1,0:T(8,128)}), f32[16,144,128]{2,1,0:T(8,128)S(1)}, u32[]{:S(2)}, u32[]{:S(2)}) %all-to-all-start) | async-done | bytes 1179680 | tf_op jit(solution)/shard_map/all_to_all | solution.py:472
  51.2 0.0 collective-permute-start.5
  51.2 22.3 %shard_map.52.d_ref = f32[2,384,384]{2,1,0:T(8,128)S(1)} custom-call(f32[16,144,128]{2,1,0:T(8,128)S(1)} %all-to-all-done.early_ref), custom_call_target="tpu_custom_call" | custom-call | flops 16999999488 | bytes 1048576 | tf_op jit(solution)/shard_map/pallas_call | solution.py:393
  73.5 0.0 copy-start.5
  73.5 1.0 copy-done.5
  74.5 0.0 collective-permute-done.5
  74.6 3.1 %collective-permute-start.7 = (f32[8,2,32,128]{3,2,1,0:T(8,128)S(1)}, f32[8,2,32,128]{3,2,1,0:T(8,128)S(1)}, u32[]{:S(2)}, u32[]{:S(2)}) collective-permute-start(f32[8,2,32,128]{3,2,1,0:T(8,128)S(1)} %pad_maximum_fusion.s1_ref), channel_id=1, source_target_pairs={{0,16},{16,0},{1,17},{17,1},{2,18},{18,2},{3,19},{19,3},{4,20},{20... | collective-permute-start | bytes 786440 | tf_op jit(solution)/shard_map/ppermute | solution.py:407
  77.7 7.6 %shard_map.53.s_ref = f32[256,256]{1,0:T(8,128)S(1)} custom-call(f32[8,2,32,128]{3,2,1,0:T(8,128)S(1)} %pad_maximum_fusion.s1_ref), custom_call_target="tpu_custom_call" | custom-call | flops 8000000000 | bytes 1048576 | tf_op jit(solution)/shard_map/pallas_call | solution.py:393
  85.3 5.7 %all-gather.3.cloned.1.call-done = f32[10752,128]{1,0:T(8,128)} async-done(((f32[672,128]{1,0:T(8,128)}), f32[10752,128]{1,0:T(8,128)}) %all-gather.3.cloned.1.call-update) | async-done | bytes 5505040 | tf_op jit(solution)/shard_map/all_gather | solution.py:469
  91.0 0.0 copy-start
  91.0 2.6 %copy-done = f32[10752,128]{1,0:T(8,128)S(1)} copy-done((f32[10752,128]{1,0:T(8,128)S(1)}, f32[10752,128]{1,0:T(8,128)}, u32[]{:S(2)}) %copy-start) | copy-done | bytes 5505048
  93.6 0.0 copy-start.1
  93.6 0.0 copy-start.6
  93.6 4.6 %shard_map.54 = (f32[96,1536]{1,0:T(8,128)S(1)}, f32[96,1536]{1,0:T(8,128)S(1)}) custom-call(s32[3]{0:T(128)S(1)} %pad_add_fusion.where_ref, f32[16,672,128]{2,1,0:T(8,128)S(1)} %bitcast.29, f32[256,256]{1,0:T(8,128)S(1)} %shard_map.53.s_ref, f32[128,1024]{1,0:T(8,128)S(1)} %get-tuple-element.21.mine_ref, f32[128,1024]{1,0:T(8,128)S(1)} %collective-permute-done.recv_ref), custom_call_target="tpu_custom_call" | custom-call | flops 3000000000 | bytes 1048576 | tf_op jit(solution)/shard_map/pallas_call | solution.py:393
  98.2 0.0 collective-permute-done.7.s1_far_ref
  98.2 0.0 copy-done.1
  98.2 0.0 copy-done.6
  98.2 38.0 %shard_map.55 = (f32[48,1536]{1,0:T(8,128)S(1)}, f32[48,1536]{1,0:T(8,128)S(1)}) custom-call(s32[3]{0:T(128)S(1)} %pad_add_fusion.where_ref, f32[16,672,128]{2,1,0:T(8,128)S(1)} %bitcast.30, f32[8,2,32,128]{3,2,1,0:T(8,128)S(1)} %pad_maximum_fusion.s1_ref, f32[8,2,32,128]{3,2,1,0:T(8,128)S(1)} %collective-permute-done.7.s1_far_ref, ...), custom_call_target="tpu_custom_call" | custom-call | flops 24999999488 | bytes 1048576 | tf_op jit(solution)/shard_map/pallas_call | solution.py:393
  136.2 0.9 collective-permute-start.8
  137.1 0.1 collective-permute-start.6
  137.2 1.1 collective-permute-done.8
  138.3 0.9 maximum_bitcast_fusion.1
  139.2 0.0 collective-permute-done.6
  139.2 0.1 select_bitcast_fusion.1
  139.3 1.1 maximum_bitcast_fusion
  (6 shorter events, 0.1 us)
Async XLA Ops:
  7.2 83.8 %all-gather.3.cloned.1.call-start = ((), (), s32[]{:S(2)}) async-start(), calls=%async_computation.1 | async-start | bytes 5849088 | tf_op jit(solution)/shard_map/all_gather | solution.py:469
  7.3 1.1 copy-start.2
  8.4 0.9 copy-start.3
  9.4 0.7 copy-start.4
  10.9 3.0 %collective-permute-start = (f32[128,1024]{1,0:T(8,128)S(1)}, f32[128,1024]{1,0:T(8,128)S(1)}, u32[]{:S(2)}, u32[]{:S(2)}) collective-permute-start(f32[128,1024]{1,0:T(8,128)S(1)} %get-tuple-element.22), channel_id=1, source_target_pairs={{0,8},{8,0},{1,9},{9,1},{2,10},{10,2},{3,11},{11,3},{4,12},{12,4},... | collective-permute-start | bytes 1572872 | tf_op jit(solution)/shard_map/ppermute | solution.py:407
  16.0 4.8 %collective-permute-start.4 = (f32[3,48,128]{2,1,0:T(8,128)S(1)}, f32[3,48,128]{2,1,0:T(8,128)S(1)}, u32[]{:S(2)}, u32[]{:S(2)}) collective-permute-start(f32[3,48,128]{2,1,0:T(8,128)S(1)} %get-tuple-element.26), channel_id=1, source_target_pairs={{0,16},{16,0},{1,17},{17,1},{2,18},{18,2},{3,19},{19,3},{4,20},{20... | collective-permute-start | bytes 221192 | tf_op jit(solution)/shard_map/ppermute | solution.py:407
  21.9 29.3 %all-to-all-start = ((f32[16,144,128]{2,1,0:T(8,128)}), f32[16,144,128]{2,1,0:T(8,128)S(1)}, u32[]{:S(2)}, u32[]{:S(2)}) async-start(f32[16,144,128]{2,1,0:T(8,128)} %broadcast_in_dim.9), calls=%async_computation | async-start | bytes 2359296 | tf_op jit(solution)/shard_map/all_to_all | solution.py:472
  29.6 6.8 %collective-permute-start.3 = (f32[2,32,128]{2,1,0:T(8,128)S(1)}, f32[2,32,128]{2,1,0:T(8,128)S(1)}, u32[]{:S(2)}, u32[]{:S(2)}) collective-permute-start(f32[2,32,128]{2,1,0:T(8,128)S(1)} %get-tuple-element.24), channel_id=1, source_target_pairs={{0,3},{1,0},{2,1},{3,2},{4,7},{5,4},{6,5},{7,6},{8,11},{9,8},{10,9... | collective-permute-start | bytes 98312 | tf_op jit(solution)/shard_map/ppermute | solution.py:412
  32.1 5.6 %collective-permute-start.2 = (f32[2,32,128]{2,1,0:T(8,128)S(1)}, f32[2,32,128]{2,1,0:T(8,128)S(1)}, u32[]{:S(2)}, u32[]{:S(2)}) collective-permute-start(f32[2,32,128]{2,1,0:T(8,128)S(1)} %get-tuple-element.24), channel_id=1, source_target_pairs={{0,2},{1,3},{2,0},{3,1},{4,6},{5,7},{6,4},{7,5},{8,10},{9,11},{10,... | collective-permute-start | bytes 98312 | tf_op jit(solution)/shard_map/ppermute | solution.py:412
  32.7 8.6 %collective-permute-start.1 = (f32[2,32,128]{2,1,0:T(8,128)S(1)}, f32[2,32,128]{2,1,0:T(8,128)S(1)}, u32[]{:S(2)}, u32[]{:S(2)}) collective-permute-start(f32[2,32,128]{2,1,0:T(8,128)S(1)} %get-tuple-element.24), channel_id=1, source_target_pairs={{0,1},{1,2},{2,3},{3,0},{4,5},{5,6},{6,7},{7,4},{8,9},{9,10},{10,1... | collective-permute-start | bytes 98312 | tf_op jit(solution)/shard_map/ppermute | solution.py:412
  51.2 23.3 %collective-permute-start.5 = (f32[4,2,32,128]{3,2,1,0:T(8,128)S(1)}, f32[4,2,32,128]{3,2,1,0:T(8,128)S(1)}, u32[]{:S(2)}, u32[]{:S(2)}) collective-permute-start(f32[4,2,32,128]{3,2,1,0:T(8,128)S(1)} %pad_maximum_fusion.1), channel_id=1, source_target_pairs={{0,4},{4,0},{1,5},{5,1},{2,6},{6,2},{3,7},{7,3},{8,12},{12,8},{9,1... | collective-permute-start | bytes 393224 | tf_op jit(solution)/shard_map/ppermute | solution.py:407
  73.5 1.0 copy-start.5
  74.6 23.6 %collective-permute-start.7 = (f32[8,2,32,128]{3,2,1,0:T(8,128)S(1)}, f32[8,2,32,128]{3,2,1,0:T(8,128)S(1)}, u32[]{:S(2)}, u32[]{:S(2)}) collective-permute-start(f32[8,2,32,128]{3,2,1,0:T(8,128)S(1)} %pad_maximum_fusion.s1_ref), channel_id=1, source_target_pairs={{0,16},{16,0},{1,17},{17,1},{2,18},{18,2},{3,19},{19,3},{4,20},{20... | collective-permute-start | bytes 786440 | tf_op jit(solution)/shard_map/ppermute | solution.py:407
  91.0 2.6 %copy-start = (f32[10752,128]{1,0:T(8,128)S(1)}, f32[10752,128]{1,0:T(8,128)}, u32[]{:S(2)}) copy-start(f32[10752,128]{1,0:T(8,128)} %all-gather.3.cloned.1.call-done) | copy-start | bytes 16515076
  93.6 4.6 %copy-start.1 = (f32[10752,128]{1,0:T(8,128)S(1)}, f32[10752,128]{1,0:T(8,128)}, u32[]{:S(2)}) copy-start(f32[10752,128]{1,0:T(8,128)} %all-gather.3.cloned.1.call-done) | copy-start | bytes 16515076
  93.6 4.6 %copy-start.6 = (f32[2,384,384]{2,1,0:T(8,128)S(1)}, f32[2,384,384]{2,1,0:T(8,128)}, u32[]{:S(2)}) copy-start(f32[2,384,384]{2,1,0:T(8,128)} %copy-done.5) | copy-start | bytes 3538948
  136.2 2.1 %collective-permute-start.8 = (f32[48,1536]{1,0:T(8,128)S(1)}, f32[48,1536]{1,0:T(8,128)S(1)}, u32[]{:S(2)}, u32[]{:S(2)}) collective-permute-start(f32[48,1536]{1,0:T(8,128)S(1)} %get-tuple-element.39), channel_id=1, source_target_pairs={{0,8},{8,0},{1,9},{9,1},{2,10},{10,2},{3,11},{11,3},{4,12},{12,4},... | collective-permute-start | bytes 884744 | tf_op jit(solution)/shard_map/ppermute | solution.py:407
  137.1 2.1 %collective-permute-start.6 = (f32[96,1536]{1,0:T(8,128)S(1)}, f32[96,1536]{1,0:T(8,128)S(1)}, u32[]{:S(2)}, u32[]{:S(2)}) collective-permute-start(f32[96,1536]{1,0:T(8,128)S(1)} %get-tuple-element.32), channel_id=1, source_target_pairs={{0,8},{8,0},{1,9},{9,1},{2,10},{10,2},{3,11},{11,3},{4,12},{12,4},... | collective-permute-start | bytes 1769480 | tf_op jit(solution)/shard_map/ppermute | solution.py:407
Sparse Core Ops, SparseCore 0:
  16.1 74.8 all-gather.2

commit v3 on v2

--- a/solution.py
+++ b/solution.py
@@ -65,7 +65,8 @@
     return out
 
 
-def sweep_blocks(mats):
+def sweep_blocks(mats, work=()):
+    work = list(work)
     tiles, per = 16, PANEL // 8
     lane = lax.broadcasted_iota(jnp.int32, (8, 128), 1)
     sub = lax.broadcasted_iota(jnp.int32, (8, 128), 0)
@@ -97,6 +98,9 @@
                 elif t not in near:
                     new[t] = jnp.where(inblk, 0.0, rows[t]) - change[8 * t : 8 * t + 8]
             mats[c] = new
+        left = tiles // per - k
+        for _ in range(-(-len(work) // left)):
+            work.pop(0)()
     return [jnp.concatenate(rows, 0) for rows in mats]
 
 
@@ -139,16 +143,14 @@
     return shared + other
 
 
-def join_columns(panels):
-    rows = panels[0].shape[0]
+def join_pair(shared, other):
+    rows = shared.shape[0]
     index = lane_index(rows, True)
     low = lax.broadcasted_iota(jnp.int32, (rows, 128), 1) < 64
-    out = []
-    for j in range(3):
-        s, o = panels[j], panels[3 + j]
-        out.append(pick(jnp.where(low, s, pltpu.roll(o, 64, 1)), index))
-        out.append(pick(jnp.where(low, pltpu.roll(s, 64, 1), o), index))
-    return out
+    return (
+        pick(jnp.where(low, shared, pltpu.roll(other, 64, 1)), index),
+        pick(jnp.where(low, pltpu.roll(shared, 64, 1), other), index),
+    )
 
 
 def shared_rows(x):
@@ -229,77 +231,51 @@
     d_ref[...] = -d_ref[...]
 
 
-def inner_kernel(s1_ref, out_ref):
+def inner_kernel(where_ref, early_ref, mine_ref, recv_ref, left_ref, inv_ref):
+    first = where_ref[0] == 0
+    pair = where_ref[2]
     for k in range(8):
         for j in range(2):
-            out_ref[32 * k : 32 * k + 32, 128 * j : 128 * j + 128] = s1_ref[k, j]
+            inv_ref[32 * k : 32 * k + 32, 128 * j : 128 * j + 128] = early_ref[
+                8 * pair + k, 144 + 32 * j : 176 + 32 * j
+            ]
 
     def step(kb, carry):
-        sweep_refs([out_ref], kb)
+        sweep_refs([inv_ref], kb)
         return carry
 
     lax.fori_loop(0, 2, step, 0)
-    out_ref[...] = -out_ref[...]
-
-
-def one_kernel(
-    where_ref, bulk_hbm, s_ref, mine_ref, recv_ref, keep_ref, send_ref, bulk_ref, u_ref, sems
-):
-    first = where_ref[0] == 0
-    pair = where_ref[2]
-    copies = [
-        pltpu.make_async_copy(bulk_hbm.at[8 * pair + k, 0:384], bulk_ref.at[k], sems.at[k])
-        for k in range(8)
-    ]
-    for copy in copies:
-        copy.start()
-    boxes = choose(first, mine_ref[32:128, :], recv_ref[32:128, :])
-    left = jnp.concatenate([boxes[0][:, 0:256], boxes[1][:, 0:256]], 0)
-    left = dot(left, s_ref[...])
-    for k, copy in enumerate(copies):
-        copy.wait()
-        for j in range(12):
-            u_ref[32 * k : 32 * k + 32, 128 * j : 128 * j + 128] = bulk_ref[
-                k, 32 * j : 32 * j + 32
-            ]
-    right = dot(left, u_ref[...])
-    outs = []
-    for t in range(2):
-        block = right[96 * t : 96 * t + 96]
-        panels = []
-        for h in range(2):
-            part = join_columns(
-                [block[:, 768 * h + 128 * j : 768 * h + 128 * j + 128] for j in range(6)]
-            )
-            for j in range(6):
-                if h == t:
-                    panels.append(boxes[t][:, 256 + 128 * j : 384 + 128 * j] - part[j])
-                else:
-                    panels.append(-part[j])
-        outs.append(jnp.concatenate(panels, 1))
-    keep_ref[...], send_ref[...] = choose(first, outs[0], outs[1])
-
-
-def two_kernel(
+    boxes = choose(first, mine_ref[32:128, 0:256], recv_ref[32:128, 0:256])
+    left_ref[...] = -dot(jnp.concatenate(boxes, 0), inv_ref[...])
+
+
+def late_kernel(
     where_ref,
     bulk_hbm,
-    s1_ref,
-    s1_far_ref,
+    early_ref,
     d_ref,
     es_ref,
     ei_ref,
     lee_ref,
-    keep_ref,
-    send_ref,
+    left_ref,
+    mine_ref,
+    recv_ref,
+    one_keep_ref,
+    one_send_ref,
+    two_keep_ref,
+    two_send_ref,
     u_ref,
     v_ref,
     c_ref,
+    m_ref,
     l_ref,
+    t_ref,
     bulk_ref,
     sems,
 ):
     first = where_ref[0] == 0
     upper = where_ref[2] == 0
+    pair = where_ref[2]
     parts = (slice(0, 384), slice(384, 672))
     copies = [
         [
@@ -315,6 +291,10 @@
             copy.start()
     for copy in copies[0]:
         copy.wait()
+
+    def block(i):
+        return slice(128 * i, 128 * i + 128)
+
     for p in range(2):
         for k in range(8):
             at = slice(256 * p + 32 * k, 256 * p + 32 * k + 32)
@@ -324,65 +304,142 @@
                     u_ref[at, 384 * t + 128 * j : 384 * t + 128 * j + 128] = bulk_ref[
                         8 * p + k, base : base + 32
                     ]
-    for t in range(2):
-        v_ref[:, 384 * t : 384 * t + 384] = dot(u_ref[:, 384 * t : 384 * t + 384], d_ref[t])
-    c_ref[...] = -dot_nt(v_ref[...], u_ref[...])
-    for k in range(8):
-        for j in range(2):
-            for p, block in enumerate(choose(upper, s1_ref[k, j], s1_far_ref[k, j])):
-                at = (
-                    slice(256 * p + 32 * k, 256 * p + 32 * k + 32),
-                    slice(256 * p + 128 * j, 256 * p + 128 * j + 128),
+
+
+    def fill_v(i):
+        for t in range(2):
+            cols = slice(384 * t, 384 * t + 384)
+            v_ref[block(i), cols] = dot(u_ref[block(i), cols], d_ref[t])
+
+    def fill_c(i):
+        width = 128 * (i + 1)
+        c_ref[block(i), 0:width] = -dot_nt(v_ref[block(i), :], u_ref[0:width, :])
+        p = i // 2
+        for k in range(4):
+            rows = slice(128 * i + 32 * k, 128 * i + 32 * k + 32)
+            for j in range(i % 2 + 1):
+                at = 4 * (i % 2) + k
+                cols = block(2 * p + j)
+                c_ref[rows, cols] = (
+                    c_ref[rows, cols] + early_ref[8 * p + at, 144 + 32 * j : 176 + 32 * j]
                 )
-                c_ref[at] = c_ref[at] + block
-
-    def step(kb, carry):
-        sweep_refs([c_ref], kb)
-        return carry
-
-    lax.fori_loop(0, 4, step, 0)
-    blank = jnp.zeros((48, 256), jnp.float32)
-    rows, direct = [], []
-    for t in range(2):
-        low, high = choose(upper, ei_ref[t], blank)
-        placed = jnp.concatenate([low, high], 1)
-        rows.append(placed - dot_nt(es_ref[t], v_ref[:, 384 * t : 384 * t + 384]))
-        direct.append(dot(es_ref[t], d_ref[t]))
+
+    def fill_f():
+        blank = jnp.zeros((48, 256), jnp.float32)
+        for t in range(2):
+            placed = jnp.concatenate(choose(upper, ei_ref[t], blank), 1)
+            c_ref[512 + 48 * t : 560 + 48 * t, :] = placed - dot_nt(
+                es_ref[t], v_ref[:, 384 * t : 384 * t + 384]
+            )
+
+    def fill_t():
+        for t in range(2):
+            t_ref[48 * t : 48 * t + 48, 384 * t : 384 * t + 384] = dot(es_ref[t], d_ref[t])
+            t_ref[48 * t : 48 * t + 48, 384 - 384 * t : 768 - 384 * t] = jnp.zeros(
+                (48, 384), jnp.float32
+            )
+
+    def side(k, rows):
+        m_ref[rows, block(k)] = dot(c_ref[rows, block(k)], inverse[k])
+
+    def trail(k, rows, start, stop):
+        cols = slice(128 * start, 128 * stop)
+        c_ref[rows, cols] = c_ref[rows, cols] - dot_nt(m_ref[rows, block(k)], c_ref[cols, block(k)])
+
+
+    def fill_one(h, j):
+        shared = u_ref[pl.ds(pl.multiple_of(256 * pair, 256), 256), 384 * h + 128 * j : 384 * h + 128 * j + 128]
+        base = 32 * (6 * h + 3 + j)
+        other = jnp.concatenate(
+            [bulk_ref[8 * pair + k, base : base + 32] for k in range(8)], 0
+        )
+        both = dot(left_ref[...], jnp.concatenate([shared, other], 1))
+        halves = join_pair(both[:, 0:128], both[:, 128:256])
+        at = 256 * j
+        cols = slice(768 * h + at, 768 * h + at + 256)
+        rows = []
+        for t in range(2):
+            part = jnp.concatenate([half[96 * t : 96 * t + 96] for half in halves], 1)
+            if t == h:
+                natural = jnp.where(
+                    first == (t == 0),
+                    mine_ref[32:128, 256 + at : 512 + at],
+                    recv_ref[32:128, 256 + at : 512 + at],
+                )
+                rows.append(natural - part)
+            else:
+                rows.append(-part)
+        one_keep_ref[:, cols], one_send_ref[:, cols] = choose(first, rows[0], rows[1])
+
+    def wait_late():
+        for copy in copies[1]:
+            copy.wait()
+
+    def fill_l(p, t):
+        for k in range(8):
+            for j in range(3):
+                base = 384 + 144 * t + 48 * j
+                l_ref[2 * p + t, 48 * k : 48 * k + 48, 128 * j : 128 * j + 128] = bulk_ref[
+                    8 * p + k, base : base + 48
+                ]
+                base = 32 * (6 * t + 3 + j)
+                l_ref[2 * p + t, 384 + 32 * k : 416 + 32 * k, 128 * j : 128 * j + 128] = bulk_ref[
+                    8 * p + k, base : base + 32
+                ]
+
+    inverse = []
+    extra = slice(512, 608)
+    run = functools.partial
+    work = [
+        [run(fill_v, 1), run(fill_c, 1)]
+        + [run(fill_v, 2), run(fill_c, 2)]
+        + [run(fill_v, 3), run(fill_c, 3)]
+        + [fill_f, fill_t],
+        [
+            run(side, 0, slice(256, 608)),
+            run(trail, 0, block(2), 1, 3),
+            run(trail, 0, block(3), 1, 4),
+            run(trail, 0, extra, 1, 4),
+        ]
+        + [run(fill_one, 0, j) for j in range(3)],
+        [
+            run(side, 1, slice(384, 608)),
+            run(trail, 1, block(3), 2, 4),
+            run(trail, 1, extra, 2, 4),
+        ]
+        + [run(fill_one, 1, j) for j in range(3)],
+        [
+            run(side, 2, extra),
+            run(trail, 2, extra, 3, 4),
+            wait_late,
+        ]
+        + [run(fill_l, p, t) for p in range(2) for t in range(2)],
+    ]
+    fill_v(0)
+    fill_c(0)
+    for k in range(4):
+        if k:
+            side(k - 1, block(k))
+            trail(k - 1, block(k), k, k + 1)
+        (x,) = sweep_blocks([c_ref[block(k), block(k)]], work[k])
+        inverse.append(-x)
+    g = [None] * 4
+    total = t_ref[...]
+    g[3] = dot(c_ref[extra, block(3)], inverse[3])
+    for k in (2, 1, 0):
+        total = total - dot(g[k + 1], v_ref[block(k + 1), :])
+        after = jnp.concatenate(g[k + 1 :], 1)
+        g[k] = m_ref[extra, block(k)] - dot(after, m_ref[128 * (k + 1) : 512, block(k)])
+    total = total - dot(g[0], v_ref[block(0), :])
     none = jnp.zeros((48, 384), jnp.float32)
-    g = -dot(jnp.concatenate(rows, 0), c_ref[...])
-    t_s = (
-        jnp.concatenate(
-            [
-                jnp.concatenate([direct[0], none], 1),
-                jnp.concatenate([none, direct[1]], 1),
-            ],
-            0,
-        )
-        - dot(g, v_ref[...])
-    )
-    for copy in copies[1]:
-        copy.wait()
-    columns = []
     for p in range(2):
         for t in range(2):
-            for k in range(8):
-                for j in range(3):
-                    base = 384 + 144 * t + 48 * j
-                    l_ref[48 * k : 48 * k + 48, 128 * j : 128 * j + 128] = bulk_ref[
-                        8 * p + k, base : base + 48
-                    ]
-                    base = 32 * (6 * t + 3 + j)
-                    l_ref[384 + 32 * k : 416 + 32 * k, 128 * j : 128 * j + 128] = bulk_ref[
-                        8 * p + k, base : base + 32
-                    ]
-            weights = jnp.concatenate(
-                [t_s[:, 384 * t : 384 * t + 384], g[:, 256 * p : 256 * p + 256]], 1
-            )
-            own = jnp.where(where_ref[2] == p, lee_ref[t], 0.0)
+            weights = jnp.concatenate([total[:, 384 * t : 384 * t + 384], g[2 * p], g[2 * p + 1]], 1)
+            own = jnp.where(pair == p, lee_ref[t], 0.0)
             placed = jnp.concatenate([own, none] if t == 0 else [none, own], 0)
-            columns.append(placed - dot(weights, l_ref[...]))
-    out = jnp.concatenate(columns, 1)
-    keep_ref[...], send_ref[...] = choose(first, out[0:48], out[48:96])
+            out = placed - dot(weights, l_ref[2 * p + t])
+            cols = slice(384 * (2 * p + t), 384 * (2 * p + t) + 384)
+            two_keep_ref[:, cols], two_send_ref[:, cols] = choose(first, out[0:48], out[48:96])
 
 
 def call(kernel, outs, args, micros, limit, scratch=(), scalars=True, hbm=0):
@@ -405,22 +462,6 @@
 
 def swap(x, axis):
     return lax.ppermute(x, axis, [(0, 1), (1, 0)])
-
-
-def ring_gather(x):
-    z = lax.axis_index("z")
-    parts = [x] + [lax.ppermute(x, "z", [(i, (i + d) % 4) for i in range(4)]) for d in (1, 2, 3)]
-    ordered = []
-    for owner in range(4):
-        step = (z - owner) % 4
-        ordered.append(
-            jnp.where(
-                step < 2,
-                jnp.where(step == 0, parts[0], parts[1]),
-                jnp.where(step == 2, parts[2], parts[3]),
-            )
-        )
-    return jnp.stack(ordered)
 
 
 def by_slot(core, mine, other):
@@ -468,47 +509,33 @@
     )
     bulk_all = lax.all_gather(bulk, PLANE, axis=0, tiled=False)
     shared = keep + swap(away, "xh")
-    near = ring_gather(s1)
+    early = jnp.concatenate([shared.reshape(144, 128), s1.reshape(64, 128)], 0)
     early_all = lax.all_to_all(
-        jnp.broadcast_to(shared.reshape(144, 128), (16, 144, 128)), PLANE, 0, 0, tiled=False
-    )
-    near, early_all = lax.optimization_barrier((near, early_all))
-    across = swap(near, "xl")
+        jnp.broadcast_to(early, (16, 208, 128)), PLANE, 0, 0, tiled=False
+    )
     (d_inv,) = call(first_kernel, [(2, 384, 384)], [early_all], 17, 12, scalars=False)
-    low = lax.axis_index("xl") == 0
-    s1_own = jnp.concatenate(
-        [jnp.where(low, near, across), jnp.where(low, across, near)], 0
-    )
-    s1_own, d_inv = lax.optimization_barrier((s1_own, d_inv))
-    s1_far = swap(s1_own, "xh")
-    (s_inv,) = call(inner_kernel, [(256, 256)], [s1_own], 8, 8, scalars=False)
-    one_keep, one_send = call(
-        one_kernel,
-        [(96, 1536), (96, 1536)],
-        [where, bulk_all, s_inv, mine, recv],
-        3,
-        12,
-        hbm=1,
-        scratch=[floats(8, 384, 128), floats(256, 1536), pltpu.SemaphoreType.DMA((8,))],
-    )
-    one_recv = swap(one_send, "core")
-    bulk_late, one_keep = lax.optimization_barrier((bulk_all, one_keep))
-    two_keep, two_send = call(
-        two_kernel,
-        [(48, 1536), (48, 1536)],
-        [where, bulk_late, s1_own, s1_far, d_inv, es, ei, lee],
+    left, _ = call(
+        inner_kernel, [(192, 256), (256, 256)], [where, early_all, mine, recv], 8, 8
+    )
+    one_keep, one_send, two_keep, two_send = call(
+        late_kernel,
+        [(96, 1536), (96, 1536), (48, 1536), (48, 1536)],
+        [where, bulk_all, early_all, d_inv, es, ei, lee, left, mine, recv],
         25,
-        24,
+        48,
         hbm=1,
         scratch=[
             floats(512, 768),
             floats(512, 768),
-            floats(512, 512),
-            floats(640, 384),
+            floats(608, 512),
+            floats(608, 512),
+            floats(4, 640, 384),
+            floats(96, 768),
             floats(16, 672, 128),
             pltpu.SemaphoreType.DMA((32,)),
         ],
     )
+    one_recv = swap(one_send, "core")
     two_recv = swap(two_send, "core")
     return by_slot(core, one_keep, one_recv), by_slot(core, two_keep, two_recv)
 

time: 148 us -> 134 us (0.905)
  blocking collectives: 0 us -> 36.4 us
  waiting for transfers between devices: 28.1 us -> 4.64 us
  starting transfers between devices: 20 us -> 6.05 us
  Pallas kernels: 75.3 us -> 64.4 us
    all_to_all x0 -> x1, blocking collectives: none -> 36.4 us  [local(): lax.all_to_all(jnp.broadcast_to(early, (16, 208, 128)), PLANE, 0, 0, tile...]
    pallas_call x6 -> x5, Pallas kernels: 75.3 us -> 64.4 us  [call(): pl.pallas_call(kernel, out_shape=shapes, in_specs=specs, out_specs=[pl.Bl...]
    all_to_all x1 -> x0, waiting for transfers between devices: 9.82 us -> none  [local(): lax.all_to_all(jnp.broadcast_to(shared.reshape(144, 128), (16, 144, 128))...]
    ppermute x3 -> x0, waiting for transfers between devices: 8.02 us -> none  [ring_gather(): lax.ppermute(x, 'z', [(i, (i + d) % 4) for i in range(4)])]
    all_to_all x1 -> x0, starting transfers between devices: 7.68 us -> none  [local(): lax.all_to_all(jnp.broadcast_to(shared.reshape(144, 128), (16, 144, 128))...]
    all_gather x1, waiting for transfers between devices: 5.74 us -> 0.09 us  [local(): bulk_all = lax.all_gather(bulk, PLANE, axis=0, tiled=False)]
    ppermute x3 -> x0, starting transfers between devices: 3.73 us -> none  [ring_gather(): lax.ppermute(x, 'z', [(i, (i + d) % 4) for i in range(4)])]
    ppermute x6 -> x4, starting transfers between devices: 8.51 us -> 6.02 us  [swap(): return lax.ppermute(x, axis, [(0, 1), (1, 0)])]
  transfers between devices with their start and end apart: 11 -> 5, of which waited for: 8 -> 4; matrix products, arithmetic and copies ran while one was open for 1% -> 1% of each run, Pallas kernels for 23% -> 23%
where the time goes in v3:
time: 134 us
  Pallas kernels  64.4 us (48%)
  blocking collectives  36.4 us (27%)
  between operations  14.1 us (11%)
  local copies, waits for them, and re-layouts  6.1 us (5%)
  starting transfers between devices  6.05 us (5%)
  waiting for transfers between devices  4.64 us (3%)
  other arithmetic  2.19 us (2%)
    pallas_call x5, Pallas kernels, call(): pl.pallas_call(kernel, out_shape=shapes, in_specs=specs, out_specs=[pl.Bl...  64.4 us
    all_to_all x1, blocking collectives, local(): lax.all_to_all(jnp.broadcast_to(early, (16, 208, 128)), PLANE, 0, 0, tile...  36.4 us
    ppermute x4, starting transfers between devices, swap(): return lax.ppermute(x, axis, [(0, 1), (1, 0)])  6.02 us
    unnamed x16, local copies, waits for them, and re-layouts  5.99 us
    ppermute x4, waiting for transfers between devices, swap(): return lax.ppermute(x, axis, [(0, 1), (1, 0)])  4.53 us
  transfers between devices with their start and end apart: 5, of which 4 were waited for; matrix products, arithmetic and copies ran while one was open for 1% of the time, Pallas kernels for 23%

profile of v3, /device:TPU:1, one launch (start us, length us, event | category | flops | bytes accessed | tf_op | source)
XLA Modules:
  0.0 133.9 jit_solution(16289730440732733560)
XLA Ops:
  7.2 0.0 all-gather.3.cloned.1.call-start
  7.2 0.1 pad_add_fusion.where_ref
  7.3 0.0 copy-start.1
  7.3 1.1 copy-done.1
  8.4 0.0 copy-start.2
  8.4 0.9 copy-done.2
  9.4 0.0 copy-start.3
  9.4 0.7 copy-done.3
  10.1 0.8 shard_map.50
  10.9 1.5 %collective-permute-start = (f32[128,1024]{1,0:T(8,128)S(1)}, f32[128,1024]{1,0:T(8,128)S(1)}, u32[]{:S(2)}, u32[]{:S(2)}) collective-permute-start(f32[128,1024]{1,0:T(8,128)S(1)} %get-tuple-element.17), channel_id=1, source_target_pairs={{0,8},{8,0},{1,9},{9,1},{2,10},{10,2},{3,11},{11,3},{4,12},{12,4},... | collective-permute-start | bytes 1572872 | tf_op jit(solution)/shard_map/ppermute | solution.py:464
  12.4 1.5 %collective-permute-done.recv_ref = f32[128,1024]{1,0:T(8,128)S(1)} collective-permute-done((f32[128,1024]{1,0:T(8,128)S(1)}, f32[128,1024]{1,0:T(8,128)S(1)}, u32[]{:S(2)}, u32[]{:S(2)}) %collective-permute-start) | collective-permute-done | bytes 524320 | tf_op jit(solution)/shard_map/ppermute | solution.py:464
  13.9 2.0 %shard_map.51 = (f32[3,48,128]{2,1,0:T(8,128)S(1)}, f32[3,48,128]{2,1,0:T(8,128)S(1)}, f32[2,32,128]{2,1,0:T(8,128)S(1)}, f32[672,128]{1,0:T(8,128)}, f32[2,48,3...) custom-call(s32[3]{0:T(128)S(1)} %pad_add_fusion.where_ref, ...), custom_call_target="tpu_custom_call" | custom-call | flops 2000000000 | bytes 1048576 | tf_op jit(solution)/shard_map/pallas_call | solution.py:450
  15.9 0.0 all-gather.3.cloned.1.call-update
  16.0 2.9 %collective-permute-start.1 = (f32[3,48,128]{2,1,0:T(8,128)S(1)}, f32[3,48,128]{2,1,0:T(8,128)S(1)}, u32[]{:S(2)}, u32[]{:S(2)}) collective-permute-start(f32[3,48,128]{2,1,0:T(8,128)S(1)} %get-tuple-element.20), channel_id=1, source_target_pairs={{0,16},{16,0},{1,17},{17,1},{2,18},{18,2},{3,19},{19,3},{4,20},{20... | collective-permute-start | bytes 221192 | tf_op jit(solution)/shard_map/ppermute | solution.py:464
  18.9 1.9 %collective-permute-done.1 = f32[3,48,128]{2,1,0:T(8,128)S(1)} collective-permute-done((f32[3,48,128]{2,1,0:T(8,128)S(1)}, f32[3,48,128]{2,1,0:T(8,128)S(1)}, u32[]{:S(2)}, u32[]{:S(2)}) %collective-permute-start.1) | collective-permute-done | bytes 73760 | tf_op jit(solution)/shard_map/ppermute | solution.py:464
  20.8 0.1 broadcast_in_dim.9
  20.9 36.4 %all_to_all.5.early_ref = f32[16,208,128]{2,1,0:T(8,128)S(1)} all-to-all(f32[16,208,128]{2,1,0:T(8,128)S(1)} %broadcast_in_dim.9), channel_id=1, replica_groups=mesh['y'=4,'xh'=2,'core'=2,'xl'=2,'z'=4] {'xh','xl','z'}, dimensions={0} | all-to-all | bytes 3407872 | tf_op jit(solution)/shard_map/all_to_all | solution.py:513
  57.3 0.0 copy-start
  57.3 8.9 %shard_map.53 = (f32[192,256]{1,0:T(8,128)S(1)}, f32[256,256]{1,0:T(8,128)}) custom-call(s32[3]{0:T(128)S(1)} %pad_add_fusion.where_ref, f32[16,208,128]{2,1,0:T(8,128)S(1)} %all_to_all.5.early_ref, f32[128,1024]{1,0:T(8,128)S(1)} %get-tuple-element.16.mine_ref, f32[128,1024]{1,0:T(8,128)S(1)} %collective-permute-done.recv_ref), custom_call_target="tpu_custom_call" | custom-call | flops 8000000000 | bytes 1048576 | tf_op jit(solution)/shard_map/pallas_call | solution.py:450
  66.2 0.0 copy-done
  66.2 0.0 copy-start.6
  66.2 22.5 %shard_map.52.d_ref = f32[2,384,384]{2,1,0:T(8,128)S(1)} custom-call(f32[16,208,128]{2,1,0:T(8,128)S(1)} %all_to_all.5.early_ref), custom_call_target="tpu_custom_call" | custom-call | flops 16999999488 | bytes 1048576 | tf_op jit(solution)/shard_map/pallas_call | solution.py:450
  88.7 0.0 copy-done.6
  88.7 0.0 copy-start.4
  88.7 1.0 copy-done.4
  89.7 0.1 all-gather.3.cloned.1.call-done
  89.8 0.0 copy-start.5
  89.8 1.3 copy-done.5
  91.1 0.0 copy-start.7
  91.1 0.9 copy-done.7
  92.0 30.2 %shard_map.54 = (f32[96,1536]{1,0:T(8,128)S(1)}, f32[96,1536]{1,0:T(8,128)S(1)}, f32[48,1536]{1,0:T(8,128)S(1)}, f32[48,1536]{1,0:T(8,128)S(1)}) custom-call(s32[3]{0:T(128)S(1)} %pad_add_fusion.where_ref, f32[16,672,128]{2,1,0:T(8,128)} %bitcast.24, f32[16,208,128]{2,1,0:T(8,128)} %copy-done, f32[2,384,384]{2,1,0:T(8,128)S(1)} %copy-done.5, ...), custom_call_target="tpu_custom_call" | custom-call | flops 24999999488 | bytes 1048576 | tf_op jit(solution)/shard_map/pallas_call | solution.py:450
  122.2 1.5 %collective-permute-start.3 = (f32[48,1536]{1,0:T(8,128)S(1)}, f32[48,1536]{1,0:T(8,128)S(1)}, u32[]{:S(2)}, u32[]{:S(2)}) collective-permute-start(f32[48,1536]{1,0:T(8,128)S(1)} %get-tuple-element.29), channel_id=1, source_target_pairs={{0,8},{8,0},{1,9},{9,1},{2,10},{10,2},{3,11},{11,3},{4,12},{12,4},... | collective-permute-start | bytes 884744 | tf_op jit(solution)/shard_map/ppermute | solution.py:464
  123.7 0.1 collective-permute-start.2
  123.8 1.1 collective-permute-done.3
  124.9 0.1 select_bitcast_fusion.3
  125.0 0.9 maximum_bitcast_fusion.1
  125.9 0.0 collective-permute-done.2
  125.9 0.1 select_bitcast_fusion.1
  125.9 1.1 maximum_bitcast_fusion
  (2 shorter events, 0.0 us)
Async XLA Ops:
  7.2 82.6 %all-gather.3.cloned.1.call-start = ((), (), s32[]{:S(2)}) async-start(), calls=%async_computation.1 | async-start | bytes 5849088 | tf_op jit(solution)/shard_map/all_gather | solution.py:510
  7.3 1.1 copy-start.1
  8.4 0.9 copy-start.2
  9.4 0.7 copy-start.3
  10.9 3.0 %collective-permute-start = (f32[128,1024]{1,0:T(8,128)S(1)}, f32[128,1024]{1,0:T(8,128)S(1)}, u32[]{:S(2)}, u32[]{:S(2)}) collective-permute-start(f32[128,1024]{1,0:T(8,128)S(1)} %get-tuple-element.17), channel_id=1, source_target_pairs={{0,8},{8,0},{1,9},{9,1},{2,10},{10,2},{3,11},{11,3},{4,12},{12,4},... | collective-permute-start | bytes 1572872 | tf_op jit(solution)/shard_map/ppermute | solution.py:464
  16.0 4.8 %collective-permute-start.1 = (f32[3,48,128]{2,1,0:T(8,128)S(1)}, f32[3,48,128]{2,1,0:T(8,128)S(1)}, u32[]{:S(2)}, u32[]{:S(2)}) collective-permute-start(f32[3,48,128]{2,1,0:T(8,128)S(1)} %get-tuple-element.20), channel_id=1, source_target_pairs={{0,16},{16,0},{1,17},{17,1},{2,18},{18,2},{3,19},{19,3},{4,20},{20... | collective-permute-start | bytes 221192 | tf_op jit(solution)/shard_map/ppermute | solution.py:464
  57.3 8.9 %copy-start = (f32[16,208,128]{2,1,0:T(8,128)}, f32[16,208,128]{2,1,0:T(8,128)S(1)}, u32[]{:S(2)}) copy-start(f32[16,208,128]{2,1,0:T(8,128)S(1)} %all_to_all.5.early_ref) | copy-start | bytes 5111812
  66.2 22.5 %copy-start.6 = (f32[192,256]{1,0:T(8,128)}, f32[192,256]{1,0:T(8,128)S(1)}, u32[]{:S(2)}) copy-start(f32[192,256]{1,0:T(8,128)S(1)} %get-tuple-element.25.left_ref) | copy-start | bytes 589828
  88.7 1.0 copy-start.4
  89.8 1.3 copy-start.5
  91.1 0.9 copy-start.7
  122.2 2.7 %collective-permute-start.3 = (f32[48,1536]{1,0:T(8,128)S(1)}, f32[48,1536]{1,0:T(8,128)S(1)}, u32[]{:S(2)}, u32[]{:S(2)}) collective-permute-start(f32[48,1536]{1,0:T(8,128)S(1)} %get-tuple-element.29), channel_id=1, source_target_pairs={{0,8},{8,0},{1,9},{9,1},{2,10},{10,2},{3,11},{11,3},{4,12},{12,4},... | collective-permute-start | bytes 884744 | tf_op jit(solution)/shard_map/ppermute | solution.py:464
  123.7 2.1 %collective-permute-start.2 = (f32[96,1536]{1,0:T(8,128)S(1)}, f32[96,1536]{1,0:T(8,128)S(1)}, u32[]{:S(2)}, u32[]{:S(2)}) collective-permute-start(f32[96,1536]{1,0:T(8,128)S(1)} %get-tuple-element.27), channel_id=1, source_target_pairs={{0,8},{8,0},{1,9},{9,1},{2,10},{10,2},{3,11},{11,3},{4,12},{12,4},... | collective-permute-start | bytes 1769480 | tf_op jit(solution)/shard_map/ppermute | solution.py:464
Sparse Core Ops, SparseCore 0:
  16.1 73.6 all-gather.2
